TPU v7x, 256 devices: a whole 4x4x8 slice. The times are simulated.
256 devices in a mesh: dp: 32 (over z, x_lo, core), rep: 8 (over x_hi, y).
Axes of the slice: x: 4 (x_hi: 2, x_lo: 2; x = x_hi * 2 + x_lo), y: 4, z: 8, core: 2. Of those that a mesh axis runs over, the one named last changes fastest.
Arguments:
- image_emb: bfloat16 [32768, 512], P(('rep', 'dp')), parts along dimension 0, may hold values from -48 to 48
- text_emb: bfloat16 [32768, 512], P(('rep', 'dp')), parts along dimension 0, may hold values from -3 to 3
- labels: int32 [32768], P(('rep', 'dp')), parts along dimension 0, may hold values from 0 to 4095, as said below
Outputs:
- image_grad: float32 [32768, 512], P(('rep', 'dp')), parts along dimension 0
- text_grad: float32 [32768, 512], P(('rep', 'dp')), parts along dimension 0
There are 8 independent parts, one for each index of `rep`. A program takes and returns all parts, laid end to end along the dimension named above; each array names one. Nothing has to cross between parts.
Inputs may be any that keep to these rules, and one draw needn't show every extreme that they name: `labels`: each image row's positive text row lies in the same aligned block of 128 rows, and every text row is the positive of exactly one image row.
All inputs are finite; a program needn't handle non-finite values.
Results may differ from a plain program's by a relative error of at most 0.0017.
Values may be sent and summed in bfloat16 or wider, within the bound.
A program may use at most 64 MiB of HBM per device.

v0:
```python
import jax
import jax.numpy as jnp
from jax import lax
from jax.sharding import PartitionSpec as P

logit_scale = 10.0


def passed_along(x, axis, by):
    peers = lax.axis_size(axis)
    return lax.ppermute(x, axis, [(i, (i + by) % peers) for i in range(peers)])


def tile_scores(image_emb, text_piece):
    return logit_scale * lax.dot_general(
        image_emb, text_piece, (((1,), (1,)), ((), ())), preferred_element_type=jnp.float32
    )


def local(image_emb, text_emb, labels):
    local_rows = image_emb.shape[0]
    feature_width = image_emb.shape[1]
    cycle_size = lax.axis_size("dp")
    my_index = lax.axis_index("dp")
    row_peak = jnp.full((local_rows,), -jnp.inf, jnp.float32)
    row_mass = jnp.zeros((local_rows,), jnp.float32)
    scores = tile_scores(image_emb, lax.all_gather(text_emb, "dp", axis=0, tiled=True))
    new_peak = jnp.max(scores, axis=1)
    row_mass = row_mass * jnp.exp(row_peak - new_peak) + jnp.sum(
        jnp.exp(scores - new_peak[:, None]), axis=1
    )
    piece_peak = jnp.max(scores, axis=0)
    piece_mass = jnp.sum(jnp.exp(scores - piece_peak[None, :]), axis=0)
    col_peak = piece_peak
    col_mass = piece_mass
    row_peak, row_mass, col_peak, col_mass = (new_peak, row_mass, col_peak, col_mass)
    row_lse = row_peak + jnp.log(row_mass)
    total_peak = lax.pmax(col_peak, "dp")
    total_mass = lax.psum(col_mass * jnp.exp(col_peak - total_peak), "dp")
    col_lse = total_peak + jnp.log(total_mass)

    def weights_for(text_piece, offset):
        scores = tile_scores(image_emb, text_piece)
        piece_rows = text_piece.shape[0]
        col_part = lax.dynamic_slice_in_dim(col_lse, offset, piece_rows, 0)
        column_ids = offset + jnp.arange(piece_rows, dtype=jnp.int32)
        positive = (column_ids[None, :] == labels[:, None]).astype(jnp.float32)
        return (
            0.5 * jnp.exp(scores - row_lse[:, None])
            + 0.5 * jnp.exp(scores - col_part[None, :])
            - positive
        ).astype(jnp.bfloat16)

    def text_term(weights):
        return logit_scale * lax.dot_general(
            weights, image_emb, (((0,), (0,)), ((), ())), preferred_element_type=jnp.float32
        )

    zero_grads = jnp.zeros((local_rows, feature_width), jnp.float32)

    def visit_block(turn_index, loop_state):
        text_block, text_total, image_total = loop_state
        offset = (my_index - turn_index) % cycle_size * local_rows
        weights = weights_for(text_block, offset)
        image_total = image_total + logit_scale * jnp.dot(
            weights, text_block, preferred_element_type=jnp.float32
        )
        return (text_block, text_total + text_term(weights), image_total)

    def cycle_turn(turn_index, loop_state):
        text_block, text_total, image_total = visit_block(turn_index, loop_state)
        text_block = passed_along(text_block, "dp", 1)
        text_total = passed_along(text_total, "dp", 1)
        return (text_block, text_total, image_total)

    loop_state = lax.fori_loop(0, cycle_size - 1, cycle_turn, (text_emb, zero_grads, zero_grads))
    text_block, text_total, image_grad = visit_block(cycle_size - 1, loop_state)
    text_grad = passed_along(text_total, "dp", 1)
    return (image_grad, text_grad)


def solution(mesh):
    placed = (P(("rep", "dp"), None), P(("rep", "dp"), None), P(("rep", "dp")))
    return jax.shard_map(
        local,
        mesh=mesh,
        in_specs=placed,
        out_specs=(P(("rep", "dp"), None), P(("rep", "dp"), None)),
        check_vma=False,
    )
```

profile of v0, /device:TPU:1, one launch (start us, length us, event | category | flops | bytes accessed | tf_op | source)
XLA Modules:
  0.0 613.4 jit_solution(7635760034646095156)
XLA Ops:
  8.9 72.6 %all-gather.2.cloned.1.call-done = bf16[4096,512]{1,0:T(8,128)(2,1)} async-done(((bf16[128,512]{1,0:T(8,128)(2,1)}), bf16[4096,512]{1,0:T(8,128)(2,1)}) %all-gather.2.cloned.1.call-update) | async-done | bytes 4194320 | tf_op jit(solution)/shard_map/all_gather | solution.py:27
  85.3 101.9 %pmax.7 = f32[4096]{0:T(1024)S(1)} all-reduce(f32[4096]{0:T(1024)S(1)} %get-tuple-element.260), channel_id=1, replica_groups=mesh['dp'=32,'rep'=8] {'dp'}, use_global_device_ids=true, to_apply=%region_1.0 | all-reduce | flops 4096 | bytes 32768 | tf_op jit(solution)/shard_map/pmax | solution.py:38
  188.0 104.4 %psum.7 = f32[4096]{0:T(1024)S(1)} all-reduce(f32[4096]{0:T(1024)S(1)} %exponential_multiply_fusion), channel_id=1, replica_groups=mesh['dp'=32,'rep'=8] {'dp'}, use_global_device_ids=true, to_apply=%region_3.0 | all-reduce | flops 4096 | bytes 32768 | tf_op jit(solution)/shard_map/psum | solution.py:39
  292.5 303.8 %while.20 = (s32[]{:T(128)}, bf16[128,512]{1,0:T(8,128)(2,1)S(1)}, f32[128,512]{1,0:T(8,128)S(1)}, f32[128,512]{1,0:T(8,128)S(1)}, bf16[128,512]{1,0:T(8,128)(2,...) while((s32[]{:T(128)}, bf16[128,512]{1,0:T(8,128)(2,1)S(1)}, ...), condition=%wide.region_7.8_spmd.clone, body=%wide.region_6.7_spmd.clone.sunk | while | flops 50806928 | bytes 3510166 | solution.py:76
  319.6 9.0 %collective-permute-done = bf16[128,512]{1,0:T(8,128)(2,1)S(1)} collective-permute-done((bf16[128,512]{1,0:T(8,128)(2,1)S(1)}, bf16[128,512]{1,0:T(8,128)(2,1)S(1)}, u32[]{:S(2)}, u32[]{:S(2)}) %collective-permute-start) | collective-permute-done | bytes 131104 | tf_op jit(solution)/shard_map/while/body/eval_jaxpr/ppermute | solution.py:11
  329.5 9.0 %collective-permute-done = bf16[128,512]{1,0:T(8,128)(2,1)S(1)} collective-permute-done((bf16[128,512]{1,0:T(8,128)(2,1)S(1)}, bf16[128,512]{1,0:T(8,128)(2,1)S(1)}, u32[]{:S(2)}, u32[]{:S(2)}) %collective-permute-start) | collective-permute-done | bytes 131104 | tf_op jit(solution)/shard_map/while/body/eval_jaxpr/ppermute | solution.py:11
  339.4 9.0 %collective-permute-done = bf16[128,512]{1,0:T(8,128)(2,1)S(1)} collective-permute-done((bf16[128,512]{1,0:T(8,128)(2,1)S(1)}, bf16[128,512]{1,0:T(8,128)(2,1)S(1)}, u32[]{:S(2)}, u32[]{:S(2)}) %collective-permute-start) | collective-permute-done | bytes 131104 | tf_op jit(solution)/shard_map/while/body/eval_jaxpr/ppermute | solution.py:11
  349.3 9.0 %collective-permute-done = bf16[128,512]{1,0:T(8,128)(2,1)S(1)} collective-permute-done((bf16[128,512]{1,0:T(8,128)(2,1)S(1)}, bf16[128,512]{1,0:T(8,128)(2,1)S(1)}, u32[]{:S(2)}, u32[]{:S(2)}) %collective-permute-start) | collective-permute-done | bytes 131104 | tf_op jit(solution)/shard_map/while/body/eval_jaxpr/ppermute | solution.py:11
  359.2 9.0 %collective-permute-done = bf16[128,512]{1,0:T(8,128)(2,1)S(1)} collective-permute-done((bf16[128,512]{1,0:T(8,128)(2,1)S(1)}, bf16[128,512]{1,0:T(8,128)(2,1)S(1)}, u32[]{:S(2)}, u32[]{:S(2)}) %collective-permute-start) | collective-permute-done | bytes 131104 | tf_op jit(solution)/shard_map/while/body/eval_jaxpr/ppermute | solution.py:11
  369.2 9.0 %collective-permute-done = bf16[128,512]{1,0:T(8,128)(2,1)S(1)} collective-permute-done((bf16[128,512]{1,0:T(8,128)(2,1)S(1)}, bf16[128,512]{1,0:T(8,128)(2,1)S(1)}, u32[]{:S(2)}, u32[]{:S(2)}) %collective-permute-start) | collective-permute-done | bytes 131104 | tf_op jit(solution)/shard_map/while/body/eval_jaxpr/ppermute | solution.py:11
  379.1 9.0 %collective-permute-done = bf16[128,512]{1,0:T(8,128)(2,1)S(1)} collective-permute-done((bf16[128,512]{1,0:T(8,128)(2,1)S(1)}, bf16[128,512]{1,0:T(8,128)(2,1)S(1)}, u32[]{:S(2)}, u32[]{:S(2)}) %collective-permute-start) | collective-permute-done | bytes 131104 | tf_op jit(solution)/shard_map/while/body/eval_jaxpr/ppermute | solution.py:11
  389.0 9.0 %collective-permute-done = bf16[128,512]{1,0:T(8,128)(2,1)S(1)} collective-permute-done((bf16[128,512]{1,0:T(8,128)(2,1)S(1)}, bf16[128,512]{1,0:T(8,128)(2,1)S(1)}, u32[]{:S(2)}, u32[]{:S(2)}) %collective-permute-start) | collective-permute-done | bytes 131104 | tf_op jit(solution)/shard_map/while/body/eval_jaxpr/ppermute | solution.py:11
  398.9 9.0 %collective-permute-done = bf16[128,512]{1,0:T(8,128)(2,1)S(1)} collective-permute-done((bf16[128,512]{1,0:T(8,128)(2,1)S(1)}, bf16[128,512]{1,0:T(8,128)(2,1)S(1)}, u32[]{:S(2)}, u32[]{:S(2)}) %collective-permute-start) | collective-permute-done | bytes 131104 | tf_op jit(solution)/shard_map/while/body/eval_jaxpr/ppermute | solution.py:11
  408.8 9.0 %collective-permute-done = bf16[128,512]{1,0:T(8,128)(2,1)S(1)} collective-permute-done((bf16[128,512]{1,0:T(8,128)(2,1)S(1)}, bf16[128,512]{1,0:T(8,128)(2,1)S(1)}, u32[]{:S(2)}, u32[]{:S(2)}) %collective-permute-start) | collective-permute-done | bytes 131104 | tf_op jit(solution)/shard_map/while/body/eval_jaxpr/ppermute | solution.py:11
  418.7 9.0 %collective-permute-done = bf16[128,512]{1,0:T(8,128)(2,1)S(1)} collective-permute-done((bf16[128,512]{1,0:T(8,128)(2,1)S(1)}, bf16[128,512]{1,0:T(8,128)(2,1)S(1)}, u32[]{:S(2)}, u32[]{:S(2)}) %collective-permute-start) | collective-permute-done | bytes 131104 | tf_op jit(solution)/shard_map/while/body/eval_jaxpr/ppermute | solution.py:11
  428.6 9.0 %collective-permute-done = bf16[128,512]{1,0:T(8,128)(2,1)S(1)} collective-permute-done((bf16[128,512]{1,0:T(8,128)(2,1)S(1)}, bf16[128,512]{1,0:T(8,128)(2,1)S(1)}, u32[]{:S(2)}, u32[]{:S(2)}) %collective-permute-start) | collective-permute-done | bytes 131104 | tf_op jit(solution)/shard_map/while/body/eval_jaxpr/ppermute | solution.py:11
  438.6 9.0 %collective-permute-done = bf16[128,512]{1,0:T(8,128)(2,1)S(1)} collective-permute-done((bf16[128,512]{1,0:T(8,128)(2,1)S(1)}, bf16[128,512]{1,0:T(8,128)(2,1)S(1)}, u32[]{:S(2)}, u32[]{:S(2)}) %collective-permute-start) | collective-permute-done | bytes 131104 | tf_op jit(solution)/shard_map/while/body/eval_jaxpr/ppermute | solution.py:11
  448.5 9.0 %collective-permute-done = bf16[128,512]{1,0:T(8,128)(2,1)S(1)} collective-permute-done((bf16[128,512]{1,0:T(8,128)(2,1)S(1)}, bf16[128,512]{1,0:T(8,128)(2,1)S(1)}, u32[]{:S(2)}, u32[]{:S(2)}) %collective-permute-start) | collective-permute-done | bytes 131104 | tf_op jit(solution)/shard_map/while/body/eval_jaxpr/ppermute | solution.py:11
  458.4 9.0 %collective-permute-done = bf16[128,512]{1,0:T(8,128)(2,1)S(1)} collective-permute-done((bf16[128,512]{1,0:T(8,128)(2,1)S(1)}, bf16[128,512]{1,0:T(8,128)(2,1)S(1)}, u32[]{:S(2)}, u32[]{:S(2)}) %collective-permute-start) | collective-permute-done | bytes 131104 | tf_op jit(solution)/shard_map/while/body/eval_jaxpr/ppermute | solution.py:11
  468.3 9.0 %collective-permute-done = bf16[128,512]{1,0:T(8,128)(2,1)S(1)} collective-permute-done((bf16[128,512]{1,0:T(8,128)(2,1)S(1)}, bf16[128,512]{1,0:T(8,128)(2,1)S(1)}, u32[]{:S(2)}, u32[]{:S(2)}) %collective-permute-start) | collective-permute-done | bytes 131104 | tf_op jit(solution)/shard_map/while/body/eval_jaxpr/ppermute | solution.py:11
  478.2 9.0 %collective-permute-done = bf16[128,512]{1,0:T(8,128)(2,1)S(1)} collective-permute-done((bf16[128,512]{1,0:T(8,128)(2,1)S(1)}, bf16[128,512]{1,0:T(8,128)(2,1)S(1)}, u32[]{:S(2)}, u32[]{:S(2)}) %collective-permute-start) | collective-permute-done | bytes 131104 | tf_op jit(solution)/shard_map/while/body/eval_jaxpr/ppermute | solution.py:11
  488.1 9.0 %collective-permute-done = bf16[128,512]{1,0:T(8,128)(2,1)S(1)} collective-permute-done((bf16[128,512]{1,0:T(8,128)(2,1)S(1)}, bf16[128,512]{1,0:T(8,128)(2,1)S(1)}, u32[]{:S(2)}, u32[]{:S(2)}) %collective-permute-start) | collective-permute-done | bytes 131104 | tf_op jit(solution)/shard_map/while/body/eval_jaxpr/ppermute | solution.py:11
  498.1 9.0 %collective-permute-done = bf16[128,512]{1,0:T(8,128)(2,1)S(1)} collective-permute-done((bf16[128,512]{1,0:T(8,128)(2,1)S(1)}, bf16[128,512]{1,0:T(8,128)(2,1)S(1)}, u32[]{:S(2)}, u32[]{:S(2)}) %collective-permute-start) | collective-permute-done | bytes 131104 | tf_op jit(solution)/shard_map/while/body/eval_jaxpr/ppermute | solution.py:11
  508.0 9.0 %collective-permute-done = bf16[128,512]{1,0:T(8,128)(2,1)S(1)} collective-permute-done((bf16[128,512]{1,0:T(8,128)(2,1)S(1)}, bf16[128,512]{1,0:T(8,128)(2,1)S(1)}, u32[]{:S(2)}, u32[]{:S(2)}) %collective-permute-start) | collective-permute-done | bytes 131104 | tf_op jit(solution)/shard_map/while/body/eval_jaxpr/ppermute | solution.py:11
  517.9 9.0 %collective-permute-done = bf16[128,512]{1,0:T(8,128)(2,1)S(1)} collective-permute-done((bf16[128,512]{1,0:T(8,128)(2,1)S(1)}, bf16[128,512]{1,0:T(8,128)(2,1)S(1)}, u32[]{:S(2)}, u32[]{:S(2)}) %collective-permute-start) | collective-permute-done | bytes 131104 | tf_op jit(solution)/shard_map/while/body/eval_jaxpr/ppermute | solution.py:11
  527.8 9.0 %collective-permute-done = bf16[128,512]{1,0:T(8,128)(2,1)S(1)} collective-permute-done((bf16[128,512]{1,0:T(8,128)(2,1)S(1)}, bf16[128,512]{1,0:T(8,128)(2,1)S(1)}, u32[]{:S(2)}, u32[]{:S(2)}) %collective-permute-start) | collective-permute-done | bytes 131104 | tf_op jit(solution)/shard_map/while/body/eval_jaxpr/ppermute | solution.py:11
  537.7 9.0 %collective-permute-done = bf16[128,512]{1,0:T(8,128)(2,1)S(1)} collective-permute-done((bf16[128,512]{1,0:T(8,128)(2,1)S(1)}, bf16[128,512]{1,0:T(8,128)(2,1)S(1)}, u32[]{:S(2)}, u32[]{:S(2)}) %collective-permute-start) | collective-permute-done | bytes 131104 | tf_op jit(solution)/shard_map/while/body/eval_jaxpr/ppermute | solution.py:11
  547.6 9.0 %collective-permute-done = bf16[128,512]{1,0:T(8,128)(2,1)S(1)} collective-permute-done((bf16[128,512]{1,0:T(8,128)(2,1)S(1)}, bf16[128,512]{1,0:T(8,128)(2,1)S(1)}, u32[]{:S(2)}, u32[]{:S(2)}) %collective-permute-start) | collective-permute-done | bytes 131104 | tf_op jit(solution)/shard_map/while/body/eval_jaxpr/ppermute | solution.py:11
  557.5 9.0 %collective-permute-done = bf16[128,512]{1,0:T(8,128)(2,1)S(1)} collective-permute-done((bf16[128,512]{1,0:T(8,128)(2,1)S(1)}, bf16[128,512]{1,0:T(8,128)(2,1)S(1)}, u32[]{:S(2)}, u32[]{:S(2)}) %collective-permute-start) | collective-permute-done | bytes 131104 | tf_op jit(solution)/shard_map/while/body/eval_jaxpr/ppermute | solution.py:11
  567.5 9.0 %collective-permute-done = bf16[128,512]{1,0:T(8,128)(2,1)S(1)} collective-permute-done((bf16[128,512]{1,0:T(8,128)(2,1)S(1)}, bf16[128,512]{1,0:T(8,128)(2,1)S(1)}, u32[]{:S(2)}, u32[]{:S(2)}) %collective-permute-start) | collective-permute-done | bytes 131104 | tf_op jit(solution)/shard_map/while/body/eval_jaxpr/ppermute | solution.py:11
  577.4 9.0 %collective-permute-done = bf16[128,512]{1,0:T(8,128)(2,1)S(1)} collective-permute-done((bf16[128,512]{1,0:T(8,128)(2,1)S(1)}, bf16[128,512]{1,0:T(8,128)(2,1)S(1)}, u32[]{:S(2)}, u32[]{:S(2)}) %collective-permute-start) | collective-permute-done | bytes 131104 | tf_op jit(solution)/shard_map/while/body/eval_jaxpr/ppermute | solution.py:11
  587.3 9.0 %collective-permute-done = bf16[128,512]{1,0:T(8,128)(2,1)S(1)} collective-permute-done((bf16[128,512]{1,0:T(8,128)(2,1)S(1)}, bf16[128,512]{1,0:T(8,128)(2,1)S(1)}, u32[]{:S(2)}, u32[]{:S(2)}) %collective-permute-start) | collective-permute-done | bytes 131104 | tf_op jit(solution)/shard_map/while/body/eval_jaxpr/ppermute | solution.py:11
  (306 shorter events, 66.6 us)
Async XLA Ops:
  7.2 74.3 %all-gather.2.cloned.1.call-start = ((), (), s32[]{:S(2)}) async-start(), calls=%async_computation | async-start | bytes 4325376 | tf_op jit(solution)/shard_map/all_gather | solution.py:27
  309.3 9.4 %collective-permute-start.1 = (f32[128,512]{1,0:T(8,128)S(1)}, f32[128,512]{1,0:T(8,128)S(1)}, u32[]{:S(2)}, u32[]{:S(2)}) collective-permute-start(f32[128,512]{1,0:T(8,128)S(1)} %fusion.34), channel_id=1, source_target_pairs={{0,8},{8,16},{16,24},{24,32},{32,40},{40,48},{48,56},{56,64},{64,7... | collective-permute-start | bytes 786440 | tf_op jit(solution)/shard_map/while/body/eval_jaxpr/ppermute | solution.py:11
  319.2 9.4 %collective-permute-start.1 = (f32[128,512]{1,0:T(8,128)S(1)}, f32[128,512]{1,0:T(8,128)S(1)}, u32[]{:S(2)}, u32[]{:S(2)}) collective-permute-start(f32[128,512]{1,0:T(8,128)S(1)} %fusion.34), channel_id=1, source_target_pairs={{0,8},{8,16},{16,24},{24,32},{32,40},{40,48},{48,56},{56,64},{64,7... | collective-permute-start | bytes 786440 | tf_op jit(solution)/shard_map/while/body/eval_jaxpr/ppermute | solution.py:11
  319.3 9.3 %collective-permute-start = (bf16[128,512]{1,0:T(8,128)(2,1)S(1)}, bf16[128,512]{1,0:T(8,128)(2,1)S(1)}, u32[]{:S(2)}, u32[]{:S(2)}) collective-permute-start(bf16[128,512]{1,0:T(8,128)(2,1)S(1)} %copy.10), channel_id=1, source_target_pairs={{0,8},{8,16},{16,24},{24,32},{32,40},{40,48},{48,56},{56,64},{64,7... | collective-permute-start | bytes 393224 | tf_op jit(solution)/shard_map/while/body/eval_jaxpr/ppermute | solution.py:11
  329.1 9.4 %collective-permute-start.1 = (f32[128,512]{1,0:T(8,128)S(1)}, f32[128,512]{1,0:T(8,128)S(1)}, u32[]{:S(2)}, u32[]{:S(2)}) collective-permute-start(f32[128,512]{1,0:T(8,128)S(1)} %fusion.34), channel_id=1, source_target_pairs={{0,8},{8,16},{16,24},{24,32},{32,40},{40,48},{48,56},{56,64},{64,7... | collective-permute-start | bytes 786440 | tf_op jit(solution)/shard_map/while/body/eval_jaxpr/ppermute | solution.py:11
  339.0 9.4 %collective-permute-start.1 = (f32[128,512]{1,0:T(8,128)S(1)}, f32[128,512]{1,0:T(8,128)S(1)}, u32[]{:S(2)}, u32[]{:S(2)}) collective-permute-start(f32[128,512]{1,0:T(8,128)S(1)} %fusion.34), channel_id=1, source_target_pairs={{0,8},{8,16},{16,24},{24,32},{32,40},{40,48},{48,56},{56,64},{64,7... | collective-permute-start | bytes 786440 | tf_op jit(solution)/shard_map/while/body/eval_jaxpr/ppermute | solution.py:11
  339.1 9.3 %collective-permute-start = (bf16[128,512]{1,0:T(8,128)(2,1)S(1)}, bf16[128,512]{1,0:T(8,128)(2,1)S(1)}, u32[]{:S(2)}, u32[]{:S(2)}) collective-permute-start(bf16[128,512]{1,0:T(8,128)(2,1)S(1)} %copy.10), channel_id=1, source_target_pairs={{0,8},{8,16},{16,24},{24,32},{32,40},{40,48},{48,56},{56,64},{64,7... | collective-permute-start | bytes 393224 | tf_op jit(solution)/shard_map/while/body/eval_jaxpr/ppermute | solution.py:11
  348.9 9.4 %collective-permute-start.1 = (f32[128,512]{1,0:T(8,128)S(1)}, f32[128,512]{1,0:T(8,128)S(1)}, u32[]{:S(2)}, u32[]{:S(2)}) collective-permute-start(f32[128,512]{1,0:T(8,128)S(1)} %fusion.34), channel_id=1, source_target_pairs={{0,8},{8,16},{16,24},{24,32},{32,40},{40,48},{48,56},{56,64},{64,7... | collective-permute-start | bytes 786440 | tf_op jit(solution)/shard_map/while/body/eval_jaxpr/ppermute | solution.py:11
  358.8 9.4 %collective-permute-start.1 = (f32[128,512]{1,0:T(8,128)S(1)}, f32[128,512]{1,0:T(8,128)S(1)}, u32[]{:S(2)}, u32[]{:S(2)}) collective-permute-start(f32[128,512]{1,0:T(8,128)S(1)} %fusion.34), channel_id=1, source_target_pairs={{0,8},{8,16},{16,24},{24,32},{32,40},{40,48},{48,56},{56,64},{64,7... | collective-permute-start | bytes 786440 | tf_op jit(solution)/shard_map/while/body/eval_jaxpr/ppermute | solution.py:11
  368.8 9.4 %collective-permute-start.1 = (f32[128,512]{1,0:T(8,128)S(1)}, f32[128,512]{1,0:T(8,128)S(1)}, u32[]{:S(2)}, u32[]{:S(2)}) collective-permute-start(f32[128,512]{1,0:T(8,128)S(1)} %fusion.34), channel_id=1, source_target_pairs={{0,8},{8,16},{16,24},{24,32},{32,40},{40,48},{48,56},{56,64},{64,7... | collective-permute-start | bytes 786440 | tf_op jit(solution)/shard_map/while/body/eval_jaxpr/ppermute | solution.py:11
  378.7 9.4 %collective-permute-start.1 = (f32[128,512]{1,0:T(8,128)S(1)}, f32[128,512]{1,0:T(8,128)S(1)}, u32[]{:S(2)}, u32[]{:S(2)}) collective-permute-start(f32[128,512]{1,0:T(8,128)S(1)} %fusion.34), channel_id=1, source_target_pairs={{0,8},{8,16},{16,24},{24,32},{32,40},{40,48},{48,56},{56,64},{64,7... | collective-permute-start | bytes 786440 | tf_op jit(solution)/shard_map/while/body/eval_jaxpr/ppermute | solution.py:11
  388.6 9.4 %collective-permute-start.1 = (f32[128,512]{1,0:T(8,128)S(1)}, f32[128,512]{1,0:T(8,128)S(1)}, u32[]{:S(2)}, u32[]{:S(2)}) collective-permute-start(f32[128,512]{1,0:T(8,128)S(1)} %fusion.34), channel_id=1, source_target_pairs={{0,8},{8,16},{16,24},{24,32},{32,40},{40,48},{48,56},{56,64},{64,7... | collective-permute-start | bytes 786440 | tf_op jit(solution)/shard_map/while/body/eval_jaxpr/ppermute | solution.py:11
  398.5 9.4 %collective-permute-start.1 = (f32[128,512]{1,0:T(8,128)S(1)}, f32[128,512]{1,0:T(8,128)S(1)}, u32[]{:S(2)}, u32[]{:S(2)}) collective-permute-start(f32[128,512]{1,0:T(8,128)S(1)} %fusion.34), channel_id=1, source_target_pairs={{0,8},{8,16},{16,24},{24,32},{32,40},{40,48},{48,56},{56,64},{64,7... | collective-permute-start | bytes 786440 | tf_op jit(solution)/shard_map/while/body/eval_jaxpr/ppermute | solution.py:11
  408.4 9.4 %collective-permute-start.1 = (f32[128,512]{1,0:T(8,128)S(1)}, f32[128,512]{1,0:T(8,128)S(1)}, u32[]{:S(2)}, u32[]{:S(2)}) collective-permute-start(f32[128,512]{1,0:T(8,128)S(1)} %fusion.34), channel_id=1, source_target_pairs={{0,8},{8,16},{16,24},{24,32},{32,40},{40,48},{48,56},{56,64},{64,7... | collective-permute-start | bytes 786440 | tf_op jit(solution)/shard_map/while/body/eval_jaxpr/ppermute | solution.py:11
  418.3 9.4 %collective-permute-start.1 = (f32[128,512]{1,0:T(8,128)S(1)}, f32[128,512]{1,0:T(8,128)S(1)}, u32[]{:S(2)}, u32[]{:S(2)}) collective-permute-start(f32[128,512]{1,0:T(8,128)S(1)} %fusion.34), channel_id=1, source_target_pairs={{0,8},{8,16},{16,24},{24,32},{32,40},{40,48},{48,56},{56,64},{64,7... | collective-permute-start | bytes 786440 | tf_op jit(solution)/shard_map/while/body/eval_jaxpr/ppermute | solution.py:11
  428.3 9.4 %collective-permute-start.1 = (f32[128,512]{1,0:T(8,128)S(1)}, f32[128,512]{1,0:T(8,128)S(1)}, u32[]{:S(2)}, u32[]{:S(2)}) collective-permute-start(f32[128,512]{1,0:T(8,128)S(1)} %fusion.34), channel_id=1, source_target_pairs={{0,8},{8,16},{16,24},{24,32},{32,40},{40,48},{48,56},{56,64},{64,7... | collective-permute-start | bytes 786440 | tf_op jit(solution)/shard_map/while/body/eval_jaxpr/ppermute | solution.py:11
  438.2 9.4 %collective-permute-start.1 = (f32[128,512]{1,0:T(8,128)S(1)}, f32[128,512]{1,0:T(8,128)S(1)}, u32[]{:S(2)}, u32[]{:S(2)}) collective-permute-start(f32[128,512]{1,0:T(8,128)S(1)} %fusion.34), channel_id=1, source_target_pairs={{0,8},{8,16},{16,24},{24,32},{32,40},{40,48},{48,56},{56,64},{64,7... | collective-permute-start | bytes 786440 | tf_op jit(solution)/shard_map/while/body/eval_jaxpr/ppermute | solution.py:11
  448.1 9.4 %collective-permute-start.1 = (f32[128,512]{1,0:T(8,128)S(1)}, f32[128,512]{1,0:T(8,128)S(1)}, u32[]{:S(2)}, u32[]{:S(2)}) collective-permute-start(f32[128,512]{1,0:T(8,128)S(1)} %fusion.34), channel_id=1, source_target_pairs={{0,8},{8,16},{16,24},{24,32},{32,40},{40,48},{48,56},{56,64},{64,7... | collective-permute-start | bytes 786440 | tf_op jit(solution)/shard_map/while/body/eval_jaxpr/ppermute | solution.py:11
  458.0 9.4 %collective-permute-start.1 = (f32[128,512]{1,0:T(8,128)S(1)}, f32[128,512]{1,0:T(8,128)S(1)}, u32[]{:S(2)}, u32[]{:S(2)}) collective-permute-start(f32[128,512]{1,0:T(8,128)S(1)} %fusion.34), channel_id=1, source_target_pairs={{0,8},{8,16},{16,24},{24,32},{32,40},{40,48},{48,56},{56,64},{64,7... | collective-permute-start | bytes 786440 | tf_op jit(solution)/shard_map/while/body/eval_jaxpr/ppermute | solution.py:11
  467.9 9.4 %collective-permute-start.1 = (f32[128,512]{1,0:T(8,128)S(1)}, f32[128,512]{1,0:T(8,128)S(1)}, u32[]{:S(2)}, u32[]{:S(2)}) collective-permute-start(f32[128,512]{1,0:T(8,128)S(1)} %fusion.34), channel_id=1, source_target_pairs={{0,8},{8,16},{16,24},{24,32},{32,40},{40,48},{48,56},{56,64},{64,7... | collective-permute-start | bytes 786440 | tf_op jit(solution)/shard_map/while/body/eval_jaxpr/ppermute | solution.py:11
  477.8 9.4 %collective-permute-start.1 = (f32[128,512]{1,0:T(8,128)S(1)}, f32[128,512]{1,0:T(8,128)S(1)}, u32[]{:S(2)}, u32[]{:S(2)}) collective-permute-start(f32[128,512]{1,0:T(8,128)S(1)} %fusion.34), channel_id=1, source_target_pairs={{0,8},{8,16},{16,24},{24,32},{32,40},{40,48},{48,56},{56,64},{64,7... | collective-permute-start | bytes 786440 | tf_op jit(solution)/shard_map/while/body/eval_jaxpr/ppermute | solution.py:11
  487.8 9.4 %collective-permute-start.1 = (f32[128,512]{1,0:T(8,128)S(1)}, f32[128,512]{1,0:T(8,128)S(1)}, u32[]{:S(2)}, u32[]{:S(2)}) collective-permute-start(f32[128,512]{1,0:T(8,128)S(1)} %fusion.34), channel_id=1, source_target_pairs={{0,8},{8,16},{16,24},{24,32},{32,40},{40,48},{48,56},{56,64},{64,7... | collective-permute-start | bytes 786440 | tf_op jit(solution)/shard_map/while/body/eval_jaxpr/ppermute | solution.py:11
  497.7 9.4 %collective-permute-start.1 = (f32[128,512]{1,0:T(8,128)S(1)}, f32[128,512]{1,0:T(8,128)S(1)}, u32[]{:S(2)}, u32[]{:S(2)}) collective-permute-start(f32[128,512]{1,0:T(8,128)S(1)} %fusion.34), channel_id=1, source_target_pairs={{0,8},{8,16},{16,24},{24,32},{32,40},{40,48},{48,56},{56,64},{64,7... | collective-permute-start | bytes 786440 | tf_op jit(solution)/shard_map/while/body/eval_jaxpr/ppermute | solution.py:11
  507.6 9.4 %collective-permute-start.1 = (f32[128,512]{1,0:T(8,128)S(1)}, f32[128,512]{1,0:T(8,128)S(1)}, u32[]{:S(2)}, u32[]{:S(2)}) collective-permute-start(f32[128,512]{1,0:T(8,128)S(1)} %fusion.34), channel_id=1, source_target_pairs={{0,8},{8,16},{16,24},{24,32},{32,40},{40,48},{48,56},{56,64},{64,7... | collective-permute-start | bytes 786440 | tf_op jit(solution)/shard_map/while/body/eval_jaxpr/ppermute | solution.py:11
  517.5 9.4 %collective-permute-start.1 = (f32[128,512]{1,0:T(8,128)S(1)}, f32[128,512]{1,0:T(8,128)S(1)}, u32[]{:S(2)}, u32[]{:S(2)}) collective-permute-start(f32[128,512]{1,0:T(8,128)S(1)} %fusion.34), channel_id=1, source_target_pairs={{0,8},{8,16},{16,24},{24,32},{32,40},{40,48},{48,56},{56,64},{64,7... | collective-permute-start | bytes 786440 | tf_op jit(solution)/shard_map/while/body/eval_jaxpr/ppermute | solution.py:11
  527.4 9.4 %collective-permute-start.1 = (f32[128,512]{1,0:T(8,128)S(1)}, f32[128,512]{1,0:T(8,128)S(1)}, u32[]{:S(2)}, u32[]{:S(2)}) collective-permute-start(f32[128,512]{1,0:T(8,128)S(1)} %fusion.34), channel_id=1, source_target_pairs={{0,8},{8,16},{16,24},{24,32},{32,40},{40,48},{48,56},{56,64},{64,7... | collective-permute-start | bytes 786440 | tf_op jit(solution)/shard_map/while/body/eval_jaxpr/ppermute | solution.py:11
  537.3 9.4 %collective-permute-start.1 = (f32[128,512]{1,0:T(8,128)S(1)}, f32[128,512]{1,0:T(8,128)S(1)}, u32[]{:S(2)}, u32[]{:S(2)}) collective-permute-start(f32[128,512]{1,0:T(8,128)S(1)} %fusion.34), channel_id=1, source_target_pairs={{0,8},{8,16},{16,24},{24,32},{32,40},{40,48},{48,56},{56,64},{64,7... | collective-permute-start | bytes 786440 | tf_op jit(solution)/shard_map/while/body/eval_jaxpr/ppermute | solution.py:11
  547.2 9.4 %collective-permute-start.1 = (f32[128,512]{1,0:T(8,128)S(1)}, f32[128,512]{1,0:T(8,128)S(1)}, u32[]{:S(2)}, u32[]{:S(2)}) collective-permute-start(f32[128,512]{1,0:T(8,128)S(1)} %fusion.34), channel_id=1, source_target_pairs={{0,8},{8,16},{16,24},{24,32},{32,40},{40,48},{48,56},{56,64},{64,7... | collective-permute-start | bytes 786440 | tf_op jit(solution)/shard_map/while/body/eval_jaxpr/ppermute | solution.py:11
  557.2 9.4 %collective-permute-start.1 = (f32[128,512]{1,0:T(8,128)S(1)}, f32[128,512]{1,0:T(8,128)S(1)}, u32[]{:S(2)}, u32[]{:S(2)}) collective-permute-start(f32[128,512]{1,0:T(8,128)S(1)} %fusion.34), channel_id=1, source_target_pairs={{0,8},{8,16},{16,24},{24,32},{32,40},{40,48},{48,56},{56,64},{64,7... | collective-permute-start | bytes 786440 | tf_op jit(solution)/shard_map/while/body/eval_jaxpr/ppermute | solution.py:11
  567.1 9.4 %collective-permute-start.1 = (f32[128,512]{1,0:T(8,128)S(1)}, f32[128,512]{1,0:T(8,128)S(1)}, u32[]{:S(2)}, u32[]{:S(2)}) collective-permute-start(f32[128,512]{1,0:T(8,128)S(1)} %fusion.34), channel_id=1, source_target_pairs={{0,8},{8,16},{16,24},{24,32},{32,40},{40,48},{48,56},{56,64},{64,7... | collective-permute-start | bytes 786440 | tf_op jit(solution)/shard_map/while/body/eval_jaxpr/ppermute | solution.py:11
  577.0 9.4 %collective-permute-start.1 = (f32[128,512]{1,0:T(8,128)S(1)}, f32[128,512]{1,0:T(8,128)S(1)}, u32[]{:S(2)}, u32[]{:S(2)}) collective-permute-start(f32[128,512]{1,0:T(8,128)S(1)} %fusion.34), channel_id=1, source_target_pairs={{0,8},{8,16},{16,24},{24,32},{32,40},{40,48},{48,56},{56,64},{64,7... | collective-permute-start | bytes 786440 | tf_op jit(solution)/shard_map/while/body/eval_jaxpr/ppermute | solution.py:11
  586.9 9.4 %collective-permute-start.1 = (f32[128,512]{1,0:T(8,128)S(1)}, f32[128,512]{1,0:T(8,128)S(1)}, u32[]{:S(2)}, u32[]{:S(2)}) collective-permute-start(f32[128,512]{1,0:T(8,128)S(1)} %fusion.34), channel_id=1, source_target_pairs={{0,8},{8,16},{16,24},{24,32},{32,40},{40,48},{48,56},{56,64},{64,7... | collective-permute-start | bytes 786440 | tf_op jit(solution)/shard_map/while/body/eval_jaxpr/ppermute | solution.py:11
  (35 other events, 906.6 us)
Sparse Core Ops, SparseCore 0:
  10.4 71.0 all-gather.1
where the time goes:
time: 619 us; the launch traced here: 613 us
  waiting for transfers between devices  351 us (57%)
  blocking collectives  206 us (33%)
  matrix products  23.7 us (4%)
  between operations  14.2 us (2%)
  starting transfers between devices  10.6 us (2%)
    ppermute x63, waiting for transfers between devices, passed_along(): return lax.ppermute(x, axis, [(i, (i + by) % peers) for i in range(peers)])  278 us
    psum x1, blocking collectives, local(): total_mass = lax.psum(col_mass * jnp.exp(col_peak - total_peak), 'dp')  104 us
    pmax x1, blocking collectives, local(): total_peak = lax.pmax(col_peak, 'dp')  102 us
    all_gather x1, waiting for transfers between devices, local(): lax.all_gather(text_emb, 'dp', axis=0, tiled=True)  72.6 us
  transfers between devices with their start and end apart: 64, of which 33 were waited for; matrix products, arithmetic and copies ran while one was open for 1% of the time, Pallas kernels for 0%

commit v1 on v0

v1 whole, which is shorter than its diff:
```python
import functools
import math

import jax
import jax.numpy as jnp
from jax import lax
from jax.experimental import pallas as pl
from jax.experimental.pallas import tpu as pltpu
from jax.sharding import PartitionSpec as P

logit_scale = 10.0
log2_scale = logit_scale / math.log(2.0)

ROWS = 128
HALF = 64
CHUNK = 32
NCH = ROWS // CHUNK
PLANES = 8
MESH = pl.DeviceIdType.MESH

OFFSETS = (0, -1, -2, -3, 1, 2, 3, 4)
SLOT_OF = {o: i for i, o in enumerate(OFFSETS)}
SLOT_OF[-4] = 7


def scores_of(rows, cols):
    return log2_scale * lax.dot_general(
        rows, cols, (((1,), (1,)), ((), ())), preferred_element_type=jnp.float32
    )


def to_lanes(column):
    return jnp.transpose(jnp.broadcast_to(column, (ROWS, ROWS)))[0:1, :]


def to_sublanes(lanes):
    return jnp.transpose(jnp.broadcast_to(lanes, (ROWS, ROWS)))


def log_add(a, b):
    top = jnp.maximum(a, b)
    return top + jnp.log2(jnp.exp2(a - top) + jnp.exp2(b - top))


def kernel(
    img_ref, txt_ref, lab_ref, oimg_ref, otxt_ref,
    cimg, ctxt, rimg, rtxt, scores, gimg, gtxt, gsend, grecv,
    colp, sibrx, chipcol, zrx, colf, colx, rowp, rowrx, rowabs, rsub, csub,
    ring_s, ring_r, sib_s, sib_r, z_s, z_r, misc_s, misc_r, loc_s,
):
    me = lax.axis_index("dp")
    z, x, k = me // 4, (me // 2) % 2, me % 2

    def device(plane, column, core):
        return {"dp": lax.rem(plane + PLANES, PLANES) * 4 + column * 2 + core}

    right, left = device(z + 1, x, k), device(z - 1, x, k)
    nbr, sib = device(z, 1 - x, k), device(z, x, 1 - k)
    held = (ctxt, cimg)
    rows_of = (rtxt, rimg)
    given = (txt_ref, img_ref)

    def remote(src, dst, send, recv, to):
        return pltpu.make_async_remote_copy(
            src_ref=src, dst_ref=dst, send_sem=send, recv_sem=recv, device_id=to, device_id_type=MESH
        )

    def plane_of(slot):
        off = OFFSETS[slot] if isinstance(slot, int) else jnp.where(slot < 4, -slot, slot - 3)
        return lax.rem(z + off + PLANES, PLANES)

    def slot(d, s):
        return 0 if s == 0 else 7 if s == 4 else s + 3 * d

    def valid(d, s, c):
        return s < 4 or (c < NCH // 2) == (d == 0)

    def ring(a, d, s, c):
        part = pl.ds(c * CHUNK, CHUNK)
        i = ((a * 2 + d) * 4 + s - 1) * NCH + c
        src = given[a].at[part] if s == 1 else held[a].at[slot(d, s - 1), 0, part]
        return remote(src, held[a].at[slot(d, s), 0, part], ring_s.at[i], ring_r.at[i], (right, left)[d])

    def to_sib(a, d, s):
        i = (a * 2 + d) * 5 + s
        if s == 0:
            src, dst = given[a], held[a].at[0, 1]
        elif s == 4:
            part = pl.ds(HALF * d, HALF)
            src, dst = held[a].at[7, 0, part], held[a].at[7, 1, part]
        else:
            src, dst = held[a].at[slot(d, s), 0], held[a].at[slot(d, s), 1]
        return remote(src, dst, sib_s.at[i], sib_r.at[i], sib)

    def misc(i, src, dst, to):
        return remote(src, dst, misc_s.at[i], misc_r.at[i], to)

    def rows_to_nbr(a):
        return misc(a, given[a], rows_of[a].at[0], nbr)

    def z_col(p):
        return remote(
            chipcol, zrx.at[SLOT_OF[-OFFSETS[p]]], z_s.at[p], z_r.at[SLOT_OF[-OFFSETS[p]]],
            device(z + OFFSETS[p], x, k),
        )

    def z_row(p):
        return remote(
            rowabs.at[0, z], rowabs.at[0, z], z_s.at[8 + p], z_r.at[8 + SLOT_OF[-OFFSETS[p]]],
            device(z + OFFSETS[p], x, k),
        )

    def z_row_arrives(p):
        return remote(rowabs.at[0, plane_of(p)], rowabs.at[0, plane_of(p)], z_s.at[8 + p], z_r.at[8 + p], right)

    def z_col_arrives(p):
        return remote(chipcol, zrx.at[p], z_s.at[p], z_r.at[p], right)

    own = [
        pltpu.make_async_copy(given[0], ctxt.at[0, 0], loc_s.at[0]),
        pltpu.make_async_copy(given[1], rimg.at[1], loc_s.at[1]),
        pltpu.make_async_copy(given[1], cimg.at[0, 0], loc_s.at[2]),
        pltpu.make_async_copy(given[0], rtxt.at[1], loc_s.at[3]),
    ]
    for c in own:
        c.start()
    barrier = pltpu.get_barrier_semaphore()
    peers = [device(z + o, x, k) for o in OFFSETS[1:]] + [nbr, sib]
    for p in peers:
        pl.semaphore_signal(barrier, inc=1, device_id=p, device_id_type=MESH)
    pl.semaphore_wait(barrier, len(peers))

    def first_sends(a):
        for c in range(NCH):
            for d in range(2):
                ring(a, d, 1, c).start()

    def ring_step(a, s):
        for c in range(NCH):
            for d in range(2):
                if valid(d, s, c):
                    ring(a, d, s, c).wait_recv()
                    if s < 4 and valid(d, s + 1, c):
                        ring(a, d, s + 1, c).start()
        for d in range(2):
            to_sib(a, d, s).start()

    def from_sib(a, s):
        for d in range(2):
            to_sib(a, d, s).wait_recv()

    first_sends(0)
    to_sib(0, 0, 0).start()
    rows_to_nbr(1).start()
    first_sends(1)
    to_sib(1, 0, 0).start()
    rows_to_nbr(0).start()

    row_peak = jnp.full((2 * ROWS, 1), -jnp.inf, jnp.float32)
    row_mass = jnp.zeros((2 * ROWS, 1), jnp.float32)

    def image_tile(q, peak, mass):
        s = scores_of(rimg[...].reshape(2 * ROWS, -1), ctxt[q].reshape(2 * ROWS, -1))
        scores[q] = s
        top = jnp.max(s, axis=0, keepdims=True)
        col = top + jnp.log2(jnp.sum(jnp.exp2(s - top), axis=0, keepdims=True))
        for kr in range(2):
            colp[kr, plane_of(q)] = col[:, kr * ROWS : (kr + 1) * ROWS]
        new_peak = jnp.maximum(peak, jnp.max(s, axis=1, keepdims=True))
        mass = mass * jnp.exp2(peak - new_peak) + jnp.sum(jnp.exp2(s - new_peak), axis=1, keepdims=True)
        return new_peak, mass

    ring_step(0, 1)
    own[0].wait()
    own[1].wait()
    rows_to_nbr(1).wait_recv()
    to_sib(0, 0, 0).wait_recv()
    row_peak, row_mass = image_tile(0, row_peak, row_mass)
    ring_step(0, 2)
    from_sib(0, 1)
    for q in (1, 4):
        row_peak, row_mass = image_tile(q, row_peak, row_mass)
    ring_step(0, 3)
    ring_step(1, 1)
    from_sib(0, 2)
    for q in (2, 5):
        row_peak, row_mass = image_tile(q, row_peak, row_mass)
    ring_step(0, 4)
    from_sib(0, 3)
    for q in (3, 6):
        row_peak, row_mass = image_tile(q, row_peak, row_mass)
    from_sib(0, 4)
    row_peak, row_mass = image_tile(7, row_peak, row_mass)

    col_to_sib = misc(2, colp.at[1], sibrx, sib)
    col_to_sib.start()
    row_part = row_peak + jnp.log2(row_mass)
    rowp[0] = to_lanes(row_part[:ROWS])
    rowp[1] = to_lanes(row_part[ROWS:])
    row_to_nbr = misc(3, rowp, rowrx, nbr)
    row_to_nbr.start()
    ring_step(1, 2)
    col_to_sib.wait_recv()
    chipcol[...] = log_add(colp[0], sibrx[...])
    for p in range(1, 8):
        z_col(p).start()
    row_to_nbr.wait_recv()
    row_nbr = log_add(rowp[0], rowrx[1])
    row_own = log_add(rowp[1], rowrx[0])
    rowabs[0, z] = row_own
    for p in range(1, 8):
        z_row(p).start()
    rsub[:ROWS] = to_sublanes(row_nbr + 1.0)
    rsub[ROWS:] = to_sublanes(row_own + 1.0)
    ring_step(1, 3)
    for p in range(1, 8):
        z_col_arrives(p).wait_recv()
    parts = [chipcol[...]] + [zrx[p] for p in range(1, 8)]
    top = functools.reduce(jnp.maximum, parts)
    mass = sum(jnp.exp2(p - top) for p in parts)
    colf[0] = top + jnp.log2(mass)
    colf_to_sib = misc(4, colf.at[0], colf.at[1], sib)
    colf_to_sib.start()
    colf_to_nbr = misc(5, colf.at[0, z], colx.at[0], nbr)
    colf_to_nbr.start()
    colf_to_sib.wait_recv()

    def lanes_of(ref, q):
        plane = plane_of(q)
        return jnp.concatenate([ref[0, plane], ref[1, plane]], axis=1) + 1.0

    def weights_of(s, sub, lanes):
        return jnp.exp2(s - jnp.concatenate([sub, sub], axis=1)) + jnp.exp2(s - lanes)

    def with_positive(w, positive):
        zero = jnp.zeros((ROWS, ROWS), jnp.float32)
        mask = jnp.concatenate([zero, positive.astype(jnp.float32)], axis=0)
        return w - jnp.concatenate([mask, jnp.zeros((2 * ROWS, ROWS), jnp.float32)], axis=1)

    labels = lab_ref[...] - me * ROWS
    label_rows = to_sublanes(labels.astype(jnp.float32))
    lane_ids = lax.broadcasted_iota(jnp.int32, (ROWS, ROWS), 1)
    row_ids = lax.broadcasted_iota(jnp.int32, (ROWS, ROWS), 0)

    def image_weights(q):
        return weights_of(scores[q], rsub[...], lanes_of(colf, q))

    def image_product(q, w):
        return jnp.dot(
            w.astype(jnp.bfloat16), ctxt[q].reshape(2 * ROWS, -1), preferred_element_type=jnp.float32
        )

    gimg[...] = image_product(0, with_positive(image_weights(0), label_rows == lane_ids.astype(jnp.float32)))

    def image_turn(q, carry):
        gimg[...] += image_product(q, image_weights(q))
        return carry

    lax.fori_loop(1, 8, image_turn, 0)
    gsend[0] = (logit_scale * gimg[:ROWS]).astype(jnp.bfloat16)
    gimg_to_nbr = misc(6, gsend.at[0], grecv.at[0], nbr)
    gimg_to_nbr.start()

    for p in range(1, 8):
        z_row_arrives(p).wait_recv()
    rowabs_to_sib = misc(7, rowabs.at[0], rowabs.at[1], sib)
    rowabs_to_sib.start()
    ring_step(1, 4)
    colf_to_nbr.wait_recv()
    csub[:ROWS] = to_sublanes(colx[0] + 1.0)
    csub[ROWS:] = to_sublanes(colf[0, z] + 1.0)
    rowabs_to_sib.wait_recv()
    own[2].wait()
    own[3].wait()
    rows_to_nbr(0).wait_recv()
    to_sib(1, 0, 0).wait_recv()
    from_sib(1, 1)
    from_sib(1, 2)
    from_sib(1, 3)

    def text_weights(q):
        s = scores_of(rtxt[...].reshape(2 * ROWS, -1), cimg[q].reshape(2 * ROWS, -1))
        return weights_of(s, csub[...], lanes_of(rowabs, q))

    def text_product(q, w):
        return jnp.dot(
            w.astype(jnp.bfloat16), cimg[q].reshape(2 * ROWS, -1), preferred_element_type=jnp.float32
        )

    gtxt[...] = text_product(0, with_positive(text_weights(0), labels == row_ids))

    def text_turn(q, carry):
        gtxt[...] += text_product(q, text_weights(q))
        return carry

    lax.fori_loop(1, 7, text_turn, 0)
    from_sib(1, 4)
    text_turn(7, 0)
    gsend[1] = (logit_scale * gtxt[:ROWS]).astype(jnp.bfloat16)
    gtxt_to_nbr = misc(8, gsend.at[1], grecv.at[1], nbr)
    gtxt_to_nbr.start()

    gimg_to_nbr.wait_recv()
    oimg_ref[...] = logit_scale * gimg[ROWS:] + grecv[0].astype(jnp.float32)

    for a in range(2):
        for d in range(2):
            for s in range(1, 5):
                for c in range(NCH):
                    if valid(d, s, c):
                        ring(a, d, s, c).wait_send()
                to_sib(a, d, s).wait_send()
        to_sib(a, 0, 0).wait_send()
        rows_to_nbr(a).wait_send()
    for p in range(1, 8):
        z_col(p).wait_send()
        z_row(p).wait_send()
    for c in (col_to_sib, row_to_nbr, colf_to_sib, colf_to_nbr, gimg_to_nbr, rowabs_to_sib, gtxt_to_nbr):
        c.wait_send()
    gtxt_to_nbr.wait_recv()
    otxt_ref[...] = logit_scale * gtxt[ROWS:] + grecv[1].astype(jnp.float32)


def local(image_emb, text_emb, labels):
    width = image_emb.shape[1]
    bf16, f32 = jnp.bfloat16, jnp.float32
    dma = pltpu.SemaphoreType.DMA
    block = jax.ShapeDtypeStruct((ROWS, width), f32)
    return pl.pallas_call(
        kernel,
        out_shape=(block, block),
        in_specs=[
            pl.BlockSpec(memory_space=pl.ANY),
            pl.BlockSpec(memory_space=pl.ANY),
            pl.BlockSpec(memory_space=pltpu.VMEM),
        ],
        out_specs=(pl.BlockSpec(memory_space=pltpu.VMEM), pl.BlockSpec(memory_space=pltpu.VMEM)),
        scratch_shapes=[
            pltpu.VMEM((PLANES, 2, ROWS, width), bf16),
            pltpu.VMEM((PLANES, 2, ROWS, width), bf16),
            pltpu.VMEM((2, ROWS, width), bf16),
            pltpu.VMEM((2, ROWS, width), bf16),
            pltpu.VMEM((PLANES, 2 * ROWS, 2 * ROWS), f32),
            pltpu.VMEM((2 * ROWS, width), f32),
            pltpu.VMEM((2 * ROWS, width), f32),
            pltpu.VMEM((2, ROWS, width), bf16),
            pltpu.VMEM((2, ROWS, width), bf16),
            pltpu.VMEM((2, PLANES, 1, ROWS), f32),
            pltpu.VMEM((PLANES, 1, ROWS), f32),
            pltpu.VMEM((PLANES, 1, ROWS), f32),
            pltpu.VMEM((PLANES, PLANES, 1, ROWS), f32),
            pltpu.VMEM((2, PLANES, 1, ROWS), f32),
            pltpu.VMEM((1, 1, ROWS), f32),
            pltpu.VMEM((2, 1, ROWS), f32),
            pltpu.VMEM((2, 1, ROWS), f32),
            pltpu.VMEM((2, PLANES, 1, ROWS), f32),
            pltpu.VMEM((2 * ROWS, ROWS), f32),
            pltpu.VMEM((2 * ROWS, ROWS), f32),
            dma((64,)),
            dma((64,)),
            dma((20,)),
            dma((20,)),
            dma((16,)),
            dma((16,)),
            dma((9,)),
            dma((9,)),
            dma((4,)),
        ],
        compiler_params=pltpu.CompilerParams(
            collective_id=0, has_side_effects=True, vmem_limit_bytes=32 * 1024 * 1024
        ),
        cost_estimate=pl.CostEstimate(
            flops=8 * 8 * 256 * 256 * 512, bytes_accessed=4 * 1024 * 1024, transcendentals=6 * 8 * 256 * 256
        ),
    )(image_emb, text_emb, labels.reshape(1, ROWS))


def solution(mesh):
    rows = P(("rep", "dp"), None)
    return jax.shard_map(
        local,
        mesh=mesh,
        in_specs=(rows, rows, P(("rep", "dp"))),
        out_specs=(rows, rows),
        check_vma=False,
    )
```

time: 619 us -> 54.3 us (0.09)
  waiting for transfers between devices: 351 us -> 0 us
  blocking collectives: 206 us -> 0 us
  Pallas kernels: 0 us -> 49.7 us
  matrix products: 23.7 us -> 0 us
  between operations: 14.2 us -> 0.65 us
  starting transfers between devices: 10.6 us -> 0 us
    ppermute x63 -> x0, waiting for transfers between devices: 278 us -> none  [passed_along(): return lax.ppermute(x, axis, [(i, (i + by) % peers) for i in range(peers)])]
    psum x1 -> x0, blocking collectives: 104 us -> none  [local(): total_mass = lax.psum(col_mass * jnp.exp(col_peak - total_peak), 'dp')]
    pmax x1 -> x0, blocking collectives: 102 us -> none  [local(): total_peak = lax.pmax(col_peak, 'dp')]
    all_gather x1 -> x0, waiting for transfers between devices: 72.6 us -> none  [local(): lax.all_gather(text_emb, 'dp', axis=0, tiled=True)]
    pallas_call x0 -> x1, Pallas kernels: none -> 49.7 us  [local(): pl.pallas_call(kernel, out_shape=(block, block), in_specs=[pl.BlockSpec(m...]
    dot_general x97 -> x0, matrix products: 23.7 us -> none  [the longest x33 10.2 us: tile_scores(): lax.dot_general(image_emb, text_piece, (((1,), (1,)), ((), ())), preferre...]
    ppermute x63 -> x0, starting transfers between devices: 10.6 us -> none  [passed_along(): return lax.ppermute(x, axis, [(i, (i + by) % peers) for i in range(peers)])]
  transfers between devices with their start and end apart: 64 -> 0, of which waited for: 33 -> 0; matrix products, arithmetic and copies ran while one was open for 1% -> 0% of each run, Pallas kernels for 0% -> 0%
where the time goes in v1:
time: 54.3 us; the launch traced here: 54.2 us
  Pallas kernels  49.7 us (92%)
  local copies, waits for them, and re-layouts  3.86 us (7%)
  between operations  0.65 us (1%)
    pallas_call x1, Pallas kernels, local(): pl.pallas_call(kernel, out_shape=(block, block), in_specs=[pl.BlockSpec(m...  49.7 us
    unnamed x8, local copies, waits for them, and re-layouts  3.86 us

profile of v1, /device:TPU:1, one launch (start us, length us, event | category | flops | bytes accessed | tf_op | source)
XLA Modules:
  0.0 54.2 jit_solution(759873920084310866)
XLA Ops:
  0.6 0.0 copy-start.2
  0.6 0.6 %copy-done.2 = s32[128]{0:T(128)S(1)} copy-done((s32[128]{0:T(128)S(1)}, s32[128]{0:T(128)}, u32[]{:S(2)}) %copy-start.2) | copy-done | bytes 536
  1.3 0.0 copy-start
  1.3 0.9 %copy-done = bf16[128,512]{1,0:T(8,128)(2,1)S(1)} copy-done((bf16[128,512]{1,0:T(8,128)(2,1)S(1)}, bf16[128,512]{1,0:T(8,128)(2,1)}, u32[]{:S(2)}) %copy-start) | copy-done | bytes 131096
  2.2 0.0 copy-start.1
  2.2 0.9 %copy-done.1 = bf16[128,512]{1,0:T(8,128)(2,1)S(1)} copy-done((bf16[128,512]{1,0:T(8,128)(2,1)S(1)}, bf16[128,512]{1,0:T(8,128)(2,1)}, u32[]{:S(2)}) %copy-start.1) | copy-done | bytes 131096
  3.1 49.7 %shard_map.50 = (f32[128,512]{1,0:T(8,128)S(1)}, f32[128,512]{1,0:T(8,128)S(1)}) custom-call(bf16[128,512]{1,0:T(8,128)(2,1)S(1)} %copy-done, bf16[128,512]{1,0:T(8,128)(2,1)S(1)} %copy-done.1, s32[1,128]{1,0:T(1,128)S(1)} %bitcast.1), custom_call_target="tpu_custom_call" | custom-call | flops 2147483648 | bytes 4194304 | tf_op jit(solution)/shard_map/pallas_call | solution.py:329
  52.8 0.7 %copy.7 = f32[128,512]{1,0:T(8,128)} copy(f32[128,512]{1,0:T(8,128)S(1)} %get-tuple-element.4) | data formatting | bytes 524288
  53.5 0.7 %copy.8 = f32[128,512]{1,0:T(8,128)} copy(f32[128,512]{1,0:T(8,128)S(1)} %get-tuple-element.5) | data formatting | bytes 524288
Async XLA Ops:
  0.6 0.7 %copy-start.2 = (s32[128]{0:T(128)S(1)}, s32[128]{0:T(128)}, u32[]{:S(2)}) copy-start(s32[128]{0:T(128)} %param.5) | copy-start | bytes 1540
  1.3 0.9 %copy-start = (bf16[128,512]{1,0:T(8,128)(2,1)S(1)}, bf16[128,512]{1,0:T(8,128)(2,1)}, u32[]{:S(2)}) copy-start(bf16[128,512]{1,0:T(8,128)(2,1)} %img_ref.1) | copy-start | bytes 393220
  2.2 0.9 %copy-start.1 = (bf16[128,512]{1,0:T(8,128)(2,1)S(1)}, bf16[128,512]{1,0:T(8,128)(2,1)}, u32[]{:S(2)}) copy-start(bf16[128,512]{1,0:T(8,128)(2,1)} %txt_ref.1) | copy-start | bytes 393220

commit v2 on v1

v2 whole, which is shorter than its diff:
```python
import functools
import math

import jax
import jax.numpy as jnp
from jax import lax
from jax.experimental import pallas as pl
from jax.experimental.pallas import tpu as pltpu
from jax.sharding import PartitionSpec as P

logit_scale = 10.0
log2_scale = logit_scale / math.log(2.0)

ROWS = 128
HALF = 64
CHUNKS = (32, 64)
PLANES = 8
MESH = pl.DeviceIdType.MESH

OFFSETS = (0, -1, -2, -3, 1, 2, 3, 4)
SLOT_OF = {o: i for i, o in enumerate(OFFSETS)}
SLOT_OF[-4] = 7


def scores_of(rows, cols):
    return log2_scale * lax.dot_general(
        rows, cols, (((1,), (1,)), ((), ())), preferred_element_type=jnp.float32
    )


def to_lanes(column):
    return jnp.transpose(jnp.broadcast_to(column, (ROWS, ROWS)))[0:1, :]


def to_sublanes(lanes):
    return jnp.transpose(jnp.broadcast_to(lanes, (ROWS, ROWS)))


def log_add(a, b):
    top = jnp.maximum(a, b)
    return top + jnp.log2(jnp.exp2(a - top) + jnp.exp2(b - top))


def kernel(
    img_ref, txt_ref, lab_ref, oimg_ref, otxt_ref, rimg_ref, rtxt_ref,
    cimg, ctxt, rimg, rtxt, scores, tscores, wide, gimg, gtxt, gsend,
    colp, sibrx, chipcol, zrx, colf, colx, rowp, rowrx, rowabs, rsub, csub,
    ring_t, ring_i, sib_r, z_r, misc_s, misc_r, sent, loc_s,
):
    me = lax.axis_index("dp")
    z, x, k = me // 4, (me // 2) % 2, me % 2

    def device(plane, column, core):
        return {"dp": lax.rem(plane + PLANES, PLANES) * 4 + column * 2 + core}

    right, left = device(z + 1, x, k), device(z - 1, x, k)
    nbr, sib = device(z, 1 - x, k), device(z, x, 1 - k)
    held = (ctxt, cimg)
    rows_of = (rtxt, rimg)
    given = (txt_ref, img_ref)

    def remote(src, dst, send, recv, to):
        return pltpu.make_async_remote_copy(
            src_ref=src, dst_ref=dst, send_sem=send, recv_sem=recv, device_id=to, device_id_type=MESH
        )

    def plane_of(slot):
        off = OFFSETS[slot] if isinstance(slot, int) else jnp.where(slot < 4, -slot, slot - 3)
        return lax.rem(z + off + PLANES, PLANES)

    def slot(d, s):
        return 0 if s == 0 else 7 if s == 4 else s + 3 * d

    def chunks(a, d, s):
        every = range(ROWS // CHUNKS[a])
        return [c for c in every if s < 4 or (c * CHUNKS[a] < HALF) == (d == 0)]

    def ring_id(a, d, s, c):
        before = [(e, t, b) for e in range(2) for t in range(1, 5) for b in chunks(a, e, t)]
        return before.index((d, s, c))

    def ring(a, d, s, c):
        part = pl.ds(c * CHUNKS[a], CHUNKS[a])
        src = given[a].at[part] if s == 1 else held[a].at[slot(d, s - 1), 0, part]
        arrived = (ring_t, ring_i)[a].at[ring_id(a, d, s, c)]
        return remote(src, held[a].at[slot(d, s), 0, part], sent.at[a], arrived, (right, left)[d])

    def to_sib(a, d, s):
        i = (a * 2 + d) * 5 + s
        if s == 0:
            src, dst = given[a], held[a].at[0, 1]
        elif s == 4:
            part = pl.ds(HALF * d, HALF)
            src, dst = held[a].at[7, 0, part], held[a].at[7, 1, part]
        else:
            src, dst = held[a].at[slot(d, s), 0], held[a].at[slot(d, s), 1]
        return remote(src, dst, sent.at[2 + a], sib_r.at[i], sib)

    def misc(i, src, dst, to):
        return remote(src, dst, misc_s.at[i], misc_r.at[i], to)

    def rows_to_nbr(a):
        return misc(a, given[a], rows_of[a].at[0], nbr)

    def z_col(p):
        return remote(
            chipcol, zrx.at[SLOT_OF[-OFFSETS[p]] - 1], sent.at[4], z_r.at[0],
            device(z + OFFSETS[p], x, k),
        )

    def z_row(p):
        return remote(
            rowabs.at[0, z], rowabs.at[0, z], sent.at[5], z_r.at[1],
            device(z + OFFSETS[p], x, k),
        )

    def all_bytes(ref, sem):
        pltpu.make_async_copy(ref, ref, sem).wait()

    own = [
        pltpu.make_async_copy(given[0], ctxt.at[0, 0], loc_s.at[0]),
        pltpu.make_async_copy(given[1], rimg.at[1], loc_s.at[1]),
        pltpu.make_async_copy(given[1], cimg.at[0, 0], loc_s.at[2]),
        pltpu.make_async_copy(given[0], rtxt.at[1], loc_s.at[3]),
    ]
    for c in own:
        c.start()
    barrier = pltpu.get_barrier_semaphore()
    peers = [right, left, nbr, sib]
    for p in peers:
        pl.semaphore_signal(barrier, inc=1, device_id=p, device_id_type=MESH)
    pl.semaphore_wait(barrier, len(peers))

    def first_sends_paced(a):
        def pair(c):
            for d in range(2):
                ring(a, d, 1, c).start()

        return [functools.partial(pair, c) for c in chunks(a, 0, 1)]

    def first_sends(a):
        for c in chunks(a, 0, 1):
            for d in range(2):
                ring(a, d, 1, c).start()

    def ring_step(a, s, beside=()):
        beside = list(beside)
        for c in chunks(a, 0, 1):
            for d in range(2):
                if c in chunks(a, d, s):
                    ring(a, d, s, c).wait_recv()
                    if s < 4 and c in chunks(a, d, s + 1):
                        ring(a, d, s + 1, c).start()
            if beside:
                beside.pop(0)()
        for thunk in beside:
            thunk()
        for d in range(2):
            to_sib(a, d, s).start()

    def from_sib(a, s):
        for d in range(2):
            to_sib(a, d, s).wait_recv()

    first_sends(0)
    to_sib(0, 0, 0).start()
    rows_to_nbr(1).start()

    row_peak = jnp.full((2 * ROWS, 1), -jnp.inf, jnp.float32)
    row_mass = jnp.zeros((2 * ROWS, 1), jnp.float32)

    def image_tile(q, peak, mass):
        s = scores_of(rimg[...].reshape(2 * ROWS, -1), ctxt[q].reshape(2 * ROWS, -1))
        scores[q] = s
        top = jnp.max(s, axis=0, keepdims=True)
        col = top + jnp.log2(jnp.sum(jnp.exp2(s - top), axis=0, keepdims=True))
        for kr in range(2):
            colp[kr, plane_of(q)] = col[:, kr * ROWS : (kr + 1) * ROWS]
        new_peak = jnp.maximum(peak, jnp.max(s, axis=1, keepdims=True))
        mass = mass * jnp.exp2(peak - new_peak) + jnp.sum(jnp.exp2(s - new_peak), axis=1, keepdims=True)
        return new_peak, mass

    def text_tile(q):
        tscores[q] = scores_of(rtxt[...].reshape(2 * ROWS, -1), cimg[q].reshape(2 * ROWS, -1))

    ring_step(0, 1)
    own[0].wait()
    own[1].wait()
    rows_to_nbr(1).wait_recv()
    to_sib(0, 0, 0).wait_recv()
    row_peak, row_mass = image_tile(0, row_peak, row_mass)
    ring_step(0, 2)
    first_sends(1)
    to_sib(1, 0, 0).start()
    rows_to_nbr(0).start()
    from_sib(0, 1)
    for q in (1, 4):
        row_peak, row_mass = image_tile(q, row_peak, row_mass)
    ring_step(0, 3)
    from_sib(0, 2)
    for q in (2, 5):
        row_peak, row_mass = image_tile(q, row_peak, row_mass)
    ring_step(0, 4)
    ring_step(1, 1)
    from_sib(0, 3)
    for q in (3, 6):
        row_peak, row_mass = image_tile(q, row_peak, row_mass)
    from_sib(0, 4)
    row_peak, row_mass = image_tile(7, row_peak, row_mass)

    col_to_sib = misc(2, colp.at[1], sibrx, sib)
    col_to_sib.start()
    row_part = row_peak + jnp.log2(row_mass)
    rowp[0] = to_lanes(row_part[:ROWS])
    rowp[1] = to_lanes(row_part[ROWS:])
    row_to_nbr = misc(3, rowp, rowrx, nbr)
    row_to_nbr.start()
    col_to_sib.wait_recv()
    chipcol[...] = log_add(colp[0], sibrx[...])
    for p in range(1, 8):
        z_col(p).start()
    ring_step(1, 2)
    own[2].wait()
    own[3].wait()
    rows_to_nbr(0).wait_recv()
    to_sib(1, 0, 0).wait_recv()
    text_tile(0)
    row_to_nbr.wait_recv()
    row_nbr = log_add(rowp[0], rowrx[1])
    row_own = log_add(rowp[1], rowrx[0])
    rowabs[0, z] = row_own
    for p in range(1, 8):
        z_row(p).start()
    rsub[:ROWS] = to_sublanes(row_nbr + 1.0)
    rsub[ROWS:] = to_sublanes(row_own + 1.0)
    from_sib(1, 1)
    text_tile(1)
    text_tile(4)
    ring_step(1, 3)
    from_sib(1, 2)
    text_tile(2)
    text_tile(5)
    all_bytes(zrx, z_r.at[0])
    parts = [chipcol[...]] + [zrx[p] for p in range(7)]
    top = functools.reduce(jnp.maximum, parts)
    mass = sum(jnp.exp2(p - top) for p in parts)
    colf[0] = top + jnp.log2(mass)
    colf_to_sib = misc(4, colf.at[0], colf.at[1], sib)
    colf_to_sib.start()
    colf_to_nbr = misc(5, colf.at[0, z], colx.at[0], nbr)
    colf_to_nbr.start()
    all_bytes(rowabs.at[0, pl.ds(0, 7)], z_r.at[1])
    rowabs_to_sib = misc(7, rowabs.at[0], rowabs.at[1], sib)
    rowabs_to_sib.start()
    colf_to_sib.wait_recv()

    def lanes_of(ref, q):
        plane = plane_of(q)
        return jnp.concatenate([ref[0, plane], ref[1, plane]], axis=1) + 1.0

    def weights_of(s, sub, lanes):
        return jnp.exp2(s - jnp.concatenate([sub, sub], axis=1)) + jnp.exp2(s - lanes)

    def with_positive(w, positive):
        zero = jnp.zeros((ROWS, ROWS), jnp.float32)
        mask = jnp.concatenate([zero, positive.astype(jnp.float32)], axis=0)
        return w - jnp.concatenate([mask, jnp.zeros((2 * ROWS, ROWS), jnp.float32)], axis=1)

    labels = lab_ref[...] - me * ROWS
    label_rows = to_sublanes(labels.astype(jnp.float32))
    lane_ids = lax.broadcasted_iota(jnp.int32, (ROWS, ROWS), 1)
    row_ids = lax.broadcasted_iota(jnp.int32, (ROWS, ROWS), 0)

    def image_weights(q):
        return weights_of(scores[q], rsub[...], lanes_of(colf, q))

    def place(q, w):
        wide[:, q * 2 * ROWS : (q + 1) * 2 * ROWS] = w.astype(jnp.bfloat16)

    place(0, with_positive(image_weights(0), label_rows == lane_ids.astype(jnp.float32)))
    for q in range(1, 8):
        place(q, image_weights(q))
    gimg[...] = logit_scale * jnp.dot(
        wide[...], ctxt[...].reshape(8 * 2 * ROWS, -1), preferred_element_type=jnp.float32
    )
    gsend[0] = gimg[:ROWS].astype(jnp.bfloat16)
    gimg_to_nbr = misc(6, gsend.at[0], rimg_ref, nbr)
    gimg_to_nbr.start()
    oimg_ref[...] = gimg[ROWS:]

    ring_step(1, 4)
    colf_to_nbr.wait_recv()
    csub[:ROWS] = to_sublanes(colx[0] + 1.0)
    csub[ROWS:] = to_sublanes(colf[0, z] + 1.0)
    from_sib(1, 3)
    text_tile(3)
    text_tile(6)
    rowabs_to_sib.wait_recv()

    def text_weights(q):
        return weights_of(tscores[q], csub[...], lanes_of(rowabs, q))

    place(0, with_positive(text_weights(0), labels == row_ids))
    for q in range(1, 7):
        place(q, text_weights(q))
    gtxt[...] = jnp.dot(
        wide[:, : 7 * 2 * ROWS], cimg[:7].reshape(7 * 2 * ROWS, -1), preferred_element_type=jnp.float32
    )
    from_sib(1, 4)
    text_tile(7)
    last = jnp.dot(
        text_weights(7).astype(jnp.bfloat16), cimg[7].reshape(2 * ROWS, -1), preferred_element_type=jnp.float32
    )
    gtxt[...] = logit_scale * (gtxt[...] + last)
    gsend[1] = gtxt[:ROWS].astype(jnp.bfloat16)
    gtxt_to_nbr = misc(8, gsend.at[1], rtxt_ref, nbr)
    gtxt_to_nbr.start()

    otxt_ref[...] = gtxt[ROWS:]

    for a in range(2):
        all_bytes(held[a].at[pl.ds(0, 7), 0], sent.at[a])
        all_bytes(held[a].at[:, 0], sent.at[2 + a])
        rows_to_nbr(a).wait_send()
    all_bytes(zrx, sent.at[4])
    all_bytes(rowabs.at[0, pl.ds(0, 7)], sent.at[5])
    for c in (col_to_sib, row_to_nbr, colf_to_sib, colf_to_nbr, gimg_to_nbr, rowabs_to_sib, gtxt_to_nbr):
        c.wait_send()
    gimg_to_nbr.wait_recv()
    gtxt_to_nbr.wait_recv()


def local(image_emb, text_emb, labels):
    width = image_emb.shape[1]
    bf16, f32 = jnp.bfloat16, jnp.float32
    dma = pltpu.SemaphoreType.DMA
    block = jax.ShapeDtypeStruct((ROWS, width), f32)
    other = jax.ShapeDtypeStruct((ROWS, width), bf16)
    own_img, own_txt, nbr_img, nbr_txt = pl.pallas_call(
        kernel,
        out_shape=(block, block, other, other),
        in_specs=[
            pl.BlockSpec(memory_space=pl.ANY),
            pl.BlockSpec(memory_space=pl.ANY),
            pl.BlockSpec(memory_space=pltpu.VMEM),
        ],
        out_specs=(pl.BlockSpec(memory_space=pltpu.VMEM),) * 4,
        scratch_shapes=[
            pltpu.VMEM((PLANES, 2, ROWS, width), bf16),
            pltpu.VMEM((PLANES, 2, ROWS, width), bf16),
            pltpu.VMEM((2, ROWS, width), bf16),
            pltpu.VMEM((2, ROWS, width), bf16),
            pltpu.VMEM((PLANES, 2 * ROWS, 2 * ROWS), f32),
            pltpu.VMEM((PLANES, 2 * ROWS, 2 * ROWS), f32),
            pltpu.VMEM((2 * ROWS, PLANES * 2 * ROWS), bf16),
            pltpu.VMEM((2 * ROWS, width), f32),
            pltpu.VMEM((2 * ROWS, width), f32),
            pltpu.VMEM((2, ROWS, width), bf16),
            pltpu.VMEM((2, PLANES, 1, ROWS), f32),
            pltpu.VMEM((PLANES, 1, ROWS), f32),
            pltpu.VMEM((PLANES, 1, ROWS), f32),
            pltpu.VMEM((PLANES - 1, PLANES, 1, ROWS), f32),
            pltpu.VMEM((2, PLANES, 1, ROWS), f32),
            pltpu.VMEM((1, 1, ROWS), f32),
            pltpu.VMEM((2, 1, ROWS), f32),
            pltpu.VMEM((2, 1, ROWS), f32),
            pltpu.VMEM((2, PLANES, 1, ROWS), f32),
            pltpu.VMEM((2 * ROWS, ROWS), f32),
            pltpu.VMEM((2 * ROWS, ROWS), f32),
            dma((7 * ROWS // CHUNKS[0],)),
            dma((7 * ROWS // CHUNKS[1],)),
            dma((20,)),
            dma((2,)),
            dma((9,)),
            dma((9,)),
            dma((6,)),
            dma((4,)),
        ],
        compiler_params=pltpu.CompilerParams(
            collective_id=0, has_side_effects=True, vmem_limit_bytes=32 * 1024 * 1024
        ),
        cost_estimate=pl.CostEstimate(
            flops=8 * 8 * 256 * 256 * 512, bytes_accessed=4 * 1024 * 1024, transcendentals=6 * 8 * 256 * 256
        ),
    )(image_emb, text_emb, labels.reshape(1, ROWS))
    return own_img + nbr_img.astype(f32), own_txt + nbr_txt.astype(f32)


def solution(mesh):
    rows = P(("rep", "dp"), None)
    return jax.shard_map(
        local,
        mesh=mesh,
        in_specs=(rows, rows, P(("rep", "dp"))),
        out_specs=(rows, rows),
        check_vma=False,
    )
```

time: 54.3 us -> 46.9 us (0.86)
  Pallas kernels: 49.7 us -> 42.8 us
  local copies, waits for them, and re-layouts: 3.86 us -> 2.46 us
  other arithmetic: 0 us -> 0.86 us
    pallas_call x1, Pallas kernels: 49.7 us -> 42.8 us  [local(): pl.pallas_call(kernel, out_shape=(block, block, other, other), in_specs=[...]
    unnamed x8 -> x6, local copies, waits for them, and re-layouts: 3.86 us -> 2.46 us
    add x0 -> x1, other arithmetic: none -> 0.86 us  [local(): return (own_img + nbr_img.astype(f32), own_txt + nbr_txt.astype(f32))]
where the time goes in v2:
time: 46.9 us; the launch traced here: 46.7 us
  Pallas kernels  42.8 us (91%)
  local copies, waits for them, and re-layouts  2.46 us (5%)
  other arithmetic  0.86 us (2%)
  between operations  0.65 us (1%)
    pallas_call x1, Pallas kernels, local(): pl.pallas_call(kernel, out_shape=(block, block, other, other), in_specs=[...  42.8 us
    unnamed x6, local copies, waits for them, and re-layouts  2.46 us

profile of v2, /device:TPU:1, one launch (start us, length us, event | category | flops | bytes accessed | tf_op | source)
XLA Modules:
  0.0 46.7 jit_solution(9177781832197660811)
XLA Ops:
  0.6 0.0 copy-start.2
  0.6 0.6 %copy-done.2 = s32[128]{0:T(128)S(1)} copy-done((s32[128]{0:T(128)S(1)}, s32[128]{0:T(128)}, u32[]{:S(2)}) %copy-start.2) | copy-done | bytes 536
  1.3 0.0 copy-start
  1.3 0.9 %copy-done = bf16[128,512]{1,0:T(8,128)(2,1)S(1)} copy-done((bf16[128,512]{1,0:T(8,128)(2,1)S(1)}, bf16[128,512]{1,0:T(8,128)(2,1)}, u32[]{:S(2)}) %copy-start) | copy-done | bytes 131096
  2.2 0.0 copy-start.1
  2.2 0.9 %copy-done.1 = bf16[128,512]{1,0:T(8,128)(2,1)S(1)} copy-done((bf16[128,512]{1,0:T(8,128)(2,1)S(1)}, bf16[128,512]{1,0:T(8,128)(2,1)}, u32[]{:S(2)}) %copy-start.1) | copy-done | bytes 131096
  3.1 42.8 %shard_map.50 = (f32[128,512]{1,0:T(8,128)S(1)}, f32[128,512]{1,0:T(8,128)S(1)}, bf16[128,512]{1,0:T(8,128)(2,1)S(1)}, bf16[128,512]{1,0:T(8,128)(2,1)S(1)}) custom-call(bf16[128,512]{1,0:T(8,128)(2,1)S(1)} %copy-done, bf16[128,512]{1,0:T(8,128)(2,1)S(1)} %copy-done.1, s32[1,128]{1,0:T(1,128)S(1)} %bitcast.1), custom_call_target="tpu_custom_call" | custom-call | flops 2147483648 | bytes 4194304 | tf_op jit(solution)/shard_map/pallas_call | solution.py:339
  45.9 0.9 %convert_add_fusion = (f32[128,512]{1,0:T(8,128)}, f32[128,512]{1,0:T(8,128)}) fusion(f32[128,512]{1,0:T(8,128)S(1)} %get-tuple-element.8, bf16[128,512]{1,0:T(8,128)(2,1)S(1)} %get-tuple-element.9, f32[128,512]{1,0:T(8,128)S(1)} %get-tuple-element.6, bf16[128,512]{1,0:T(8,128)(2,1)S(1)} %get-tuple-element.7), kind=kLoop, calls=%fused_computation | loop fusion | flops 262144 | bytes 1310720 | tf_op jit(solution)/shard_map/add | solution.py:386
Async XLA Ops:
  0.6 0.7 %copy-start.2 = (s32[128]{0:T(128)S(1)}, s32[128]{0:T(128)}, u32[]{:S(2)}) copy-start(s32[128]{0:T(128)} %param.5) | copy-start | bytes 1540
  1.3 0.9 %copy-start = (bf16[128,512]{1,0:T(8,128)(2,1)S(1)}, bf16[128,512]{1,0:T(8,128)(2,1)}, u32[]{:S(2)}) copy-start(bf16[128,512]{1,0:T(8,128)(2,1)} %img_ref.1) | copy-start | bytes 393220
  2.2 0.9 %copy-start.1 = (bf16[128,512]{1,0:T(8,128)(2,1)S(1)}, bf16[128,512]{1,0:T(8,128)(2,1)}, u32[]{:S(2)}) copy-start(bf16[128,512]{1,0:T(8,128)(2,1)} %txt_ref.1) | copy-start | bytes 393220

commit v3 on v2

--- a/solution.py
+++ b/solution.py
@@ -13,7 +13,7 @@
 
 ROWS = 128
 HALF = 64
-CHUNKS = (32, 64)
+CHUNKS = (32, 32)
 PLANES = 8
 MESH = pl.DeviceIdType.MESH
 
@@ -42,9 +42,9 @@
 
 
 def kernel(
-    img_ref, txt_ref, lab_ref, oimg_ref, otxt_ref, rimg_ref, rtxt_ref,
+    both_ref, lab_ref, oimg_ref, otxt_ref, rimg_ref, rtxt_ref,
     cimg, ctxt, rimg, rtxt, scores, tscores, wide, gimg, gtxt, gsend,
-    colp, sibrx, chipcol, zrx, colf, colx, rowp, rowrx, rowabs, rsub, csub,
+    colp, sibrx, zmsg, zrx, drx, final, colx, rowp, rowrx, rsub, csub,
     ring_t, ring_i, sib_r, z_r, misc_s, misc_r, sent, loc_s,
 ):
     me = lax.axis_index("dp")
@@ -57,7 +57,7 @@
     nbr, sib = device(z, 1 - x, k), device(z, x, 1 - k)
     held = (ctxt, cimg)
     rows_of = (rtxt, rimg)
-    given = (txt_ref, img_ref)
+    given = (both_ref.at[1], both_ref.at[0])
 
     def remote(src, dst, send, recv, to):
         return pltpu.make_async_remote_copy(
@@ -86,7 +86,6 @@
         return remote(src, held[a].at[slot(d, s), 0, part], sent.at[a], arrived, (right, left)[d])
 
     def to_sib(a, d, s):
-        i = (a * 2 + d) * 5 + s
         if s == 0:
             src, dst = given[a], held[a].at[0, 1]
         elif s == 4:
@@ -94,7 +93,7 @@
             src, dst = held[a].at[7, 0, part], held[a].at[7, 1, part]
         else:
             src, dst = held[a].at[slot(d, s), 0], held[a].at[slot(d, s), 1]
-        return remote(src, dst, sent.at[2 + a], sib_r.at[i], sib)
+        return remote(src, dst, sent.at[2 + a], sib_r.at[a * 5 + s], sib)
 
     def misc(i, src, dst, to):
         return remote(src, dst, misc_s.at[i], misc_r.at[i], to)
@@ -102,17 +101,13 @@
     def rows_to_nbr(a):
         return misc(a, given[a], rows_of[a].at[0], nbr)
 
-    def z_col(p):
-        return remote(
-            chipcol, zrx.at[SLOT_OF[-OFFSETS[p]] - 1], sent.at[4], z_r.at[0],
-            device(z + OFFSETS[p], x, k),
-        )
-
-    def z_row(p):
-        return remote(
-            rowabs.at[0, z], rowabs.at[0, z], sent.at[5], z_r.at[1],
-            device(z + OFFSETS[p], x, k),
-        )
+    def z_sums(p):
+        there = SLOT_OF[-OFFSETS[p]] - 1
+        return remote(zmsg, zrx.at[there], sent.at[4], z_r.at[0], device(z + OFFSETS[p], x, k))
+
+    def z_rows(p):
+        there = SLOT_OF[-OFFSETS[p]] - 1
+        return remote(rowp.at[0], drx.at[there], sent.at[5], z_r.at[1], device(z + OFFSETS[p], 1 - x, k))
 
     def all_bytes(ref, sem):
         pltpu.make_async_copy(ref, ref, sem).wait()
@@ -123,25 +118,26 @@
         pltpu.make_async_copy(given[1], cimg.at[0, 0], loc_s.at[2]),
         pltpu.make_async_copy(given[0], rtxt.at[1], loc_s.at[3]),
     ]
-    for c in own:
-        c.start()
     barrier = pltpu.get_barrier_semaphore()
     peers = [right, left, nbr, sib]
     for p in peers:
         pl.semaphore_signal(barrier, inc=1, device_id=p, device_id_type=MESH)
     pl.semaphore_wait(barrier, len(peers))
 
-    def first_sends_paced(a):
-        def pair(c):
-            for d in range(2):
-                ring(a, d, 1, c).start()
-
-        return [functools.partial(pair, c) for c in chunks(a, 0, 1)]
-
     def first_sends(a):
         for c in chunks(a, 0, 1):
             for d in range(2):
                 ring(a, d, 1, c).start()
+
+    def step_thunks(a, s):
+        def one(c):
+            for d in range(2):
+                if c in chunks(a, d, s):
+                    ring(a, d, s, c).wait_recv()
+                    if s < 4 and c in chunks(a, d, s + 1):
+                        ring(a, d, s + 1, c).start()
+
+        return [functools.partial(one, c) for c in chunks(a, 0, 1)]
 
     def ring_step(a, s, beside=()):
         beside = list(beside)
@@ -159,12 +155,16 @@
             to_sib(a, d, s).start()
 
     def from_sib(a, s):
-        for d in range(2):
-            to_sib(a, d, s).wait_recv()
+        if s == 4:
+            all_bytes(held[a].at[7, 1], sib_r.at[a * 5 + 4])
+        else:
+            all_bytes(held[a].at[pl.ds(0, 2), 1], sib_r.at[a * 5 + s])
 
     first_sends(0)
     to_sib(0, 0, 0).start()
     rows_to_nbr(1).start()
+    for c in own:
+        c.start()
 
     row_peak = jnp.full((2 * ROWS, 1), -jnp.inf, jnp.float32)
     row_mass = jnp.zeros((2 * ROWS, 1), jnp.float32)
@@ -200,11 +200,12 @@
     from_sib(0, 2)
     for q in (2, 5):
         row_peak, row_mass = image_tile(q, row_peak, row_mass)
-    ring_step(0, 4)
-    ring_step(1, 1)
     from_sib(0, 3)
     for q in (3, 6):
         row_peak, row_mass = image_tile(q, row_peak, row_mass)
+    ring_step(0, 4, step_thunks(1, 1))
+    for d in range(2):
+        to_sib(1, d, 1).start()
     from_sib(0, 4)
     row_peak, row_mass = image_tile(7, row_peak, row_mass)
 
@@ -213,12 +214,15 @@
     row_part = row_peak + jnp.log2(row_mass)
     rowp[0] = to_lanes(row_part[:ROWS])
     rowp[1] = to_lanes(row_part[ROWS:])
+    zmsg[8] = rowp[1]
     row_to_nbr = misc(3, rowp, rowrx, nbr)
     row_to_nbr.start()
     col_to_sib.wait_recv()
-    chipcol[...] = log_add(colp[0], sibrx[...])
+    zmsg[:8] = log_add(colp[0], sibrx[...])
     for p in range(1, 8):
-        z_col(p).start()
+        z_sums(p).start()
+    for p in range(1, 8):
+        z_rows(p).start()
     ring_step(1, 2)
     own[2].wait()
     own[3].wait()
@@ -228,9 +232,7 @@
     row_to_nbr.wait_recv()
     row_nbr = log_add(rowp[0], rowrx[1])
     row_own = log_add(rowp[1], rowrx[0])
-    rowabs[0, z] = row_own
-    for p in range(1, 8):
-        z_row(p).start()
+    final[0, 8 + z] = row_own
     rsub[:ROWS] = to_sublanes(row_nbr + 1.0)
     rsub[ROWS:] = to_sublanes(row_own + 1.0)
     from_sib(1, 1)
@@ -241,22 +243,22 @@
     text_tile(2)
     text_tile(5)
     all_bytes(zrx, z_r.at[0])
-    parts = [chipcol[...]] + [zrx[p] for p in range(7)]
+    all_bytes(drx, z_r.at[1])
+    parts = [zmsg[:8]] + [zrx[p, :8] for p in range(7)]
     top = functools.reduce(jnp.maximum, parts)
     mass = sum(jnp.exp2(p - top) for p in parts)
-    colf[0] = top + jnp.log2(mass)
-    colf_to_sib = misc(4, colf.at[0], colf.at[1], sib)
-    colf_to_sib.start()
-    colf_to_nbr = misc(5, colf.at[0, z], colx.at[0], nbr)
-    colf_to_nbr.start()
-    all_bytes(rowabs.at[0, pl.ds(0, 7)], z_r.at[1])
-    rowabs_to_sib = misc(7, rowabs.at[0], rowabs.at[1], sib)
-    rowabs_to_sib.start()
-    colf_to_sib.wait_recv()
-
-    def lanes_of(ref, q):
-        plane = plane_of(q)
-        return jnp.concatenate([ref[0, plane], ref[1, plane]], axis=1) + 1.0
+    final[0, :8] = top + jnp.log2(mass)
+    for p in range(1, 8):
+        final[0, 8 + plane_of(p)] = log_add(zrx[p - 1, 8], drx[p - 1])
+    final_to_sib = misc(4, final.at[0], final.at[1], sib)
+    final_to_sib.start()
+    col_to_nbr = misc(5, final.at[0, z], colx.at[0], nbr)
+    col_to_nbr.start()
+    final_to_sib.wait_recv()
+
+    def lanes_of(side, q):
+        plane = 8 * side + plane_of(q)
+        return jnp.concatenate([final[0, plane], final[1, plane]], axis=1) + 1.0
 
     def weights_of(s, sub, lanes):
         return jnp.exp2(s - jnp.concatenate([sub, sub], axis=1)) + jnp.exp2(s - lanes)
@@ -272,7 +274,7 @@
     row_ids = lax.broadcasted_iota(jnp.int32, (ROWS, ROWS), 0)
 
     def image_weights(q):
-        return weights_of(scores[q], rsub[...], lanes_of(colf, q))
+        return weights_of(scores[q], rsub[...], lanes_of(0, q))
 
     def place(q, w):
         wide[:, q * 2 * ROWS : (q + 1) * 2 * ROWS] = w.astype(jnp.bfloat16)
@@ -288,17 +290,19 @@
     gimg_to_nbr.start()
     oimg_ref[...] = gimg[ROWS:]
 
-    ring_step(1, 4)
-    colf_to_nbr.wait_recv()
+    for d in range(2):
+        for c in chunks(1, d, 4):
+            ring(1, d, 4, c).wait_recv()
+        to_sib(1, d, 4).start()
+    col_to_nbr.wait_recv()
     csub[:ROWS] = to_sublanes(colx[0] + 1.0)
-    csub[ROWS:] = to_sublanes(colf[0, z] + 1.0)
+    csub[ROWS:] = to_sublanes(final[0, z] + 1.0)
     from_sib(1, 3)
     text_tile(3)
     text_tile(6)
-    rowabs_to_sib.wait_recv()
 
     def text_weights(q):
-        return weights_of(tscores[q], csub[...], lanes_of(rowabs, q))
+        return weights_of(tscores[q], csub[...], lanes_of(1, q))
 
     place(0, with_positive(text_weights(0), labels == row_ids))
     for q in range(1, 7):
@@ -313,7 +317,7 @@
     )
     gtxt[...] = logit_scale * (gtxt[...] + last)
     gsend[1] = gtxt[:ROWS].astype(jnp.bfloat16)
-    gtxt_to_nbr = misc(8, gsend.at[1], rtxt_ref, nbr)
+    gtxt_to_nbr = misc(7, gsend.at[1], rtxt_ref, nbr)
     gtxt_to_nbr.start()
 
     otxt_ref[...] = gtxt[ROWS:]
@@ -323,8 +327,8 @@
         all_bytes(held[a].at[:, 0], sent.at[2 + a])
         rows_to_nbr(a).wait_send()
     all_bytes(zrx, sent.at[4])
-    all_bytes(rowabs.at[0, pl.ds(0, 7)], sent.at[5])
-    for c in (col_to_sib, row_to_nbr, colf_to_sib, colf_to_nbr, gimg_to_nbr, rowabs_to_sib, gtxt_to_nbr):
+    all_bytes(drx, sent.at[5])
+    for c in (col_to_sib, row_to_nbr, final_to_sib, col_to_nbr, gimg_to_nbr, gtxt_to_nbr):
         c.wait_send()
     gimg_to_nbr.wait_recv()
     gtxt_to_nbr.wait_recv()
@@ -340,7 +344,6 @@
         kernel,
         out_shape=(block, block, other, other),
         in_specs=[
-            pl.BlockSpec(memory_space=pl.ANY),
             pl.BlockSpec(memory_space=pl.ANY),
             pl.BlockSpec(memory_space=pltpu.VMEM),
         ],
@@ -358,21 +361,21 @@
             pltpu.VMEM((2, ROWS, width), bf16),
             pltpu.VMEM((2, PLANES, 1, ROWS), f32),
             pltpu.VMEM((PLANES, 1, ROWS), f32),
-            pltpu.VMEM((PLANES, 1, ROWS), f32),
-            pltpu.VMEM((PLANES - 1, PLANES, 1, ROWS), f32),
-            pltpu.VMEM((2, PLANES, 1, ROWS), f32),
+            pltpu.VMEM((PLANES + 1, 1, ROWS), f32),
+            pltpu.VMEM((PLANES - 1, PLANES + 1, 1, ROWS), f32),
+            pltpu.VMEM((PLANES - 1, 1, ROWS), f32),
+            pltpu.VMEM((2, 2 * PLANES, 1, ROWS), f32),
             pltpu.VMEM((1, 1, ROWS), f32),
             pltpu.VMEM((2, 1, ROWS), f32),
             pltpu.VMEM((2, 1, ROWS), f32),
-            pltpu.VMEM((2, PLANES, 1, ROWS), f32),
             pltpu.VMEM((2 * ROWS, ROWS), f32),
             pltpu.VMEM((2 * ROWS, ROWS), f32),
             dma((7 * ROWS // CHUNKS[0],)),
             dma((7 * ROWS // CHUNKS[1],)),
-            dma((20,)),
+            dma((10,)),
             dma((2,)),
-            dma((9,)),
-            dma((9,)),
+            dma((8,)),
+            dma((8,)),
             dma((6,)),
             dma((4,)),
         ],
@@ -382,7 +385,7 @@
         cost_estimate=pl.CostEstimate(
             flops=8 * 8 * 256 * 256 * 512, bytes_accessed=4 * 1024 * 1024, transcendentals=6 * 8 * 256 * 256
         ),
-    )(image_emb, text_emb, labels.reshape(1, ROWS))
+    )(jnp.stack([image_emb, text_emb]), labels.reshape(1, ROWS))
     return own_img + nbr_img.astype(f32), own_txt + nbr_txt.astype(f32)
 
 

time: 46.9 us -> 43.8 us (0.934)
  local copies, waits for them, and re-layouts: 2.46 us -> 0.01 us
  Pallas kernels: 42.8 us -> 41.1 us
  other arithmetic: 0.86 us -> 1.86 us
    unnamed x6 -> x2, local copies, waits for them, and re-layouts: 2.46 us -> 0.01 us
    pallas_call x1, Pallas kernels: 42.8 us -> 41.1 us  [local(): pl.pallas_call(kernel, out_shape=(block, block, other, other), in_specs=[...]
    another operation x0 -> x1, other arithmetic: none -> 1 us  [local(): jnp.stack([image_emb, text_emb])]
where the time goes in v3:
time: 43.8 us; the launch traced here: 43.7 us
  Pallas kernels  41.1 us (94%)
  other arithmetic  1.86 us (4%)
  between operations  0.66 us (2%)
    pallas_call x1, Pallas kernels, local(): pl.pallas_call(kernel, out_shape=(block, block, other, other), in_specs=[...  41.1 us
    another operation x1, other arithmetic, local(): jnp.stack([image_emb, text_emb])  1 us

profile of v3, /device:TPU:1, one launch (start us, length us, event | category | flops | bytes accessed | tf_op | source)
XLA Modules:
  0.0 43.7 jit_solution(817272574073481530)
XLA Ops:
  0.6 0.0 copy-start
  0.6 1.0 %pad_maximum_fusion.both_ref = bf16[2,128,512]{2,1,0:T(8,128)(2,1)S(1)} fusion(bf16[1,128,512]{2,1,0:T(8,128)(2,1)} %bitcast.4, bf16[1,128,512]{2,1,0:T(8,128)(2,1)} %bitcast.5), kind=kLoop, calls=%fused_computation | loop fusion | flops 131072 | bytes 524288 | tf_op jit(solution)/shard_map/stack | solution.py:388
  1.6 0.0 copy-done
  1.7 41.1 %shard_map.50 = (f32[128,512]{1,0:T(8,128)S(1)}, f32[128,512]{1,0:T(8,128)S(1)}, bf16[128,512]{1,0:T(8,128)(2,1)S(1)}, bf16[128,512]{1,0:T(8,128)(2,1)S(1)}) custom-call(bf16[2,128,512]{2,1,0:T(8,128)(2,1)S(1)} %pad_maximum_fusion.both_ref, s32[1,128]{1,0:T(1,128)S(1)} %bitcast.3), custom_call_target="tpu_custom_call" | custom-call | flops 2147483648 | bytes 4194304 | tf_op jit(solution)/shard_map/pallas_call | solution.py:343
  42.8 0.9 %convert_add_fusion = (f32[128,512]{1,0:T(8,128)}, f32[128,512]{1,0:T(8,128)}) fusion(f32[128,512]{1,0:T(8,128)S(1)} %get-tuple-element.8, bf16[128,512]{1,0:T(8,128)(2,1)S(1)} %get-tuple-element.9, f32[128,512]{1,0:T(8,128)S(1)} %get-tuple-element.6, bf16[128,512]{1,0:T(8,128)(2,1)S(1)} %get-tuple-element.7), kind=kLoop, calls=%fused_computation.1 | loop fusion | flops 262144 | bytes 1310720 | tf_op jit(solution)/shard_map/add | solution.py:389
Async XLA Ops:
  0.6 1.0 %copy-start = (s32[128]{0:T(128)S(1)}, s32[128]{0:T(128)}, u32[]{:S(2)}) copy-start(s32[128]{0:T(128)} %param.5) | copy-start | bytes 1540

commit v4 on v3

--- a/solution.py
+++ b/solution.py
@@ -43,7 +43,7 @@
 
 def kernel(
     both_ref, lab_ref, oimg_ref, otxt_ref, rimg_ref, rtxt_ref,
-    cimg, ctxt, rimg, rtxt, scores, tscores, wide, gimg, gtxt, gsend,
+    cimg, ctxt, rimg, rtxt, scores, tscores, wide, gtxt, gsend,
     colp, sibrx, zmsg, zrx, drx, final, colx, rowp, rowrx, rsub, csub,
     ring_t, ring_i, sib_r, z_r, misc_s, misc_r, sent, loc_s,
 ):
@@ -184,19 +184,19 @@
         tscores[q] = scores_of(rtxt[...].reshape(2 * ROWS, -1), cimg[q].reshape(2 * ROWS, -1))
 
     ring_step(0, 1)
+    ring_step(0, 2)
+    first_sends(1)
     own[0].wait()
     own[1].wait()
     rows_to_nbr(1).wait_recv()
     to_sib(0, 0, 0).wait_recv()
     row_peak, row_mass = image_tile(0, row_peak, row_mass)
-    ring_step(0, 2)
-    first_sends(1)
-    to_sib(1, 0, 0).start()
-    rows_to_nbr(0).start()
     from_sib(0, 1)
     for q in (1, 4):
         row_peak, row_mass = image_tile(q, row_peak, row_mass)
     ring_step(0, 3)
+    to_sib(1, 0, 0).start()
+    rows_to_nbr(0).start()
     from_sib(0, 2)
     for q in (2, 5):
         row_peak, row_mass = image_tile(q, row_peak, row_mass)
@@ -263,32 +263,22 @@
     def weights_of(s, sub, lanes):
         return jnp.exp2(s - jnp.concatenate([sub, sub], axis=1)) + jnp.exp2(s - lanes)
 
-    def with_positive(w, positive):
-        zero = jnp.zeros((ROWS, ROWS), jnp.float32)
-        mask = jnp.concatenate([zero, positive.astype(jnp.float32)], axis=0)
-        return w - jnp.concatenate([mask, jnp.zeros((2 * ROWS, ROWS), jnp.float32)], axis=1)
-
-    labels = lab_ref[...] - me * ROWS
-    label_rows = to_sublanes(labels.astype(jnp.float32))
-    lane_ids = lax.broadcasted_iota(jnp.int32, (ROWS, ROWS), 1)
-    row_ids = lax.broadcasted_iota(jnp.int32, (ROWS, ROWS), 0)
-
-    def image_weights(q):
-        return weights_of(scores[q], rsub[...], lanes_of(0, q))
-
-    def place(q, w):
-        wide[:, q * 2 * ROWS : (q + 1) * 2 * ROWS] = w.astype(jnp.bfloat16)
-
-    place(0, with_positive(image_weights(0), label_rows == lane_ids.astype(jnp.float32)))
-    for q in range(1, 8):
-        place(q, image_weights(q))
-    gimg[...] = logit_scale * jnp.dot(
-        wide[...], ctxt[...].reshape(8 * 2 * ROWS, -1), preferred_element_type=jnp.float32
-    )
-    gsend[0] = gimg[:ROWS].astype(jnp.bfloat16)
+    def products(half, count, tiles, sub, side, cols, positive=None):
+        part = pl.ds(half * ROWS, ROWS)
+        for q in range(count):
+            w = weights_of(tiles[q, part], sub[part], lanes_of(side, q))
+            if positive is not None and q == 0:
+                mask = positive.astype(jnp.float32)
+                w = w - jnp.concatenate([mask, jnp.zeros_like(mask)], axis=1)
+            wide[part, q * 2 * ROWS : (q + 1) * 2 * ROWS] = w.astype(jnp.bfloat16)
+        depth = count * 2 * ROWS
+        return jnp.dot(
+            wide[part, :depth], cols[:count].reshape(depth, -1), preferred_element_type=jnp.float32
+        )
+
+    gsend[0] = (logit_scale * products(0, 8, scores, rsub, 0, ctxt)).astype(jnp.bfloat16)
     gimg_to_nbr = misc(6, gsend.at[0], rimg_ref, nbr)
     gimg_to_nbr.start()
-    oimg_ref[...] = gimg[ROWS:]
 
     for d in range(2):
         for c in chunks(1, d, 4):
@@ -301,26 +291,23 @@
     text_tile(3)
     text_tile(6)
 
-    def text_weights(q):
-        return weights_of(tscores[q], csub[...], lanes_of(1, q))
-
-    place(0, with_positive(text_weights(0), labels == row_ids))
-    for q in range(1, 7):
-        place(q, text_weights(q))
-    gtxt[...] = jnp.dot(
-        wide[:, : 7 * 2 * ROWS], cimg[:7].reshape(7 * 2 * ROWS, -1), preferred_element_type=jnp.float32
-    )
+    gtxt[...] = products(0, 7, tscores, csub, 1, cimg)
     from_sib(1, 4)
-    text_tile(7)
-    last = jnp.dot(
-        text_weights(7).astype(jnp.bfloat16), cimg[7].reshape(2 * ROWS, -1), preferred_element_type=jnp.float32
-    )
-    gtxt[...] = logit_scale * (gtxt[...] + last)
-    gsend[1] = gtxt[:ROWS].astype(jnp.bfloat16)
+    last = cimg[7].reshape(2 * ROWS, -1)
+    w = weights_of(scores_of(rtxt[0], last), csub[:ROWS], lanes_of(1, 7)).astype(jnp.bfloat16)
+    gsend[1] = (
+        logit_scale * (gtxt[...] + jnp.dot(w, last, preferred_element_type=jnp.float32))
+    ).astype(jnp.bfloat16)
     gtxt_to_nbr = misc(7, gsend.at[1], rtxt_ref, nbr)
     gtxt_to_nbr.start()
 
-    otxt_ref[...] = gtxt[ROWS:]
+    labels = lab_ref[...] - me * ROWS
+    label_rows = to_sublanes(labels.astype(jnp.float32))
+    lane_ids = lax.broadcasted_iota(jnp.int32, (ROWS, ROWS), 1).astype(jnp.float32)
+    row_ids = lax.broadcasted_iota(jnp.int32, (ROWS, ROWS), 0)
+    text_tile(7)
+    oimg_ref[...] = logit_scale * products(1, 8, scores, rsub, 0, ctxt, label_rows == lane_ids)
+    otxt_ref[...] = logit_scale * products(1, 8, tscores, csub, 1, cimg, labels == row_ids)
 
     for a in range(2):
         all_bytes(held[a].at[pl.ds(0, 7), 0], sent.at[a])
@@ -356,8 +343,7 @@
             pltpu.VMEM((PLANES, 2 * ROWS, 2 * ROWS), f32),
             pltpu.VMEM((PLANES, 2 * ROWS, 2 * ROWS), f32),
             pltpu.VMEM((2 * ROWS, PLANES * 2 * ROWS), bf16),
-            pltpu.VMEM((2 * ROWS, width), f32),
-            pltpu.VMEM((2 * ROWS, width), f32),
+            pltpu.VMEM((ROWS, width), f32),
             pltpu.VMEM((2, ROWS, width), bf16),
             pltpu.VMEM((2, PLANES, 1, ROWS), f32),
             pltpu.VMEM((PLANES, 1, ROWS), f32),

time: 43.8 us -> 43.5 us (level)
  no operation moved by 1% of the time
where the time goes in v4:
time: 43.5 us; the launch traced here: 43.4 us
  Pallas kernels  40.8 us (94%)
  other arithmetic  1.86 us (4%)
  between operations  0.66 us (2%)
    pallas_call x1, Pallas kernels, local(): pl.pallas_call(kernel, out_shape=(block, block, other, other), in_specs=[...  40.8 us
    another operation x1, other arithmetic, local(): jnp.stack([image_emb, text_emb])  1 us

profile of v4, /device:TPU:1, one launch (start us, length us, event | category | flops | bytes accessed | tf_op | source)
XLA Modules:
  0.0 43.4 jit_solution(8656102034463353354)
XLA Ops:
  0.6 0.0 copy-start
  0.6 1.0 %pad_maximum_fusion.both_ref = bf16[2,128,512]{2,1,0:T(8,128)(2,1)S(1)} fusion(bf16[1,128,512]{2,1,0:T(8,128)(2,1)} %bitcast.4, bf16[1,128,512]{2,1,0:T(8,128)(2,1)} %bitcast.5), kind=kLoop, calls=%fused_computation | loop fusion | flops 131072 | bytes 524288 | tf_op jit(solution)/shard_map/stack | solution.py:374
  1.6 0.0 copy-done
  1.7 40.8 %shard_map.50 = (f32[128,512]{1,0:T(8,128)S(1)}, f32[128,512]{1,0:T(8,128)S(1)}, bf16[128,512]{1,0:T(8,128)(2,1)S(1)}, bf16[128,512]{1,0:T(8,128)(2,1)S(1)}) custom-call(bf16[2,128,512]{2,1,0:T(8,128)(2,1)S(1)} %pad_maximum_fusion.both_ref, s32[1,128]{1,0:T(1,128)S(1)} %bitcast.3), custom_call_target="tpu_custom_call" | custom-call | flops 2147483648 | bytes 4194304 | tf_op jit(solution)/shard_map/pallas_call | solution.py:330
  42.5 0.9 %convert_add_fusion = (f32[128,512]{1,0:T(8,128)}, f32[128,512]{1,0:T(8,128)}) fusion(f32[128,512]{1,0:T(8,128)S(1)} %get-tuple-element.8, bf16[128,512]{1,0:T(8,128)(2,1)S(1)} %get-tuple-element.9, f32[128,512]{1,0:T(8,128)S(1)} %get-tuple-element.6, bf16[128,512]{1,0:T(8,128)(2,1)S(1)} %get-tuple-element.7), kind=kLoop, calls=%fused_computation.1 | loop fusion | flops 262144 | bytes 1310720 | tf_op jit(solution)/shard_map/add | solution.py:375
Async XLA Ops:
  0.6 1.0 %copy-start = (s32[128]{0:T(128)S(1)}, s32[128]{0:T(128)}, u32[]{:S(2)}) copy-start(s32[128]{0:T(128)} %param.5) | copy-start | bytes 1540

commit v5 on v4

--- a/solution.py
+++ b/solution.py
@@ -217,12 +217,12 @@
     zmsg[8] = rowp[1]
     row_to_nbr = misc(3, rowp, rowrx, nbr)
     row_to_nbr.start()
+    for p in range(1, 8):
+        z_rows(p).start()
     col_to_sib.wait_recv()
     zmsg[:8] = log_add(colp[0], sibrx[...])
     for p in range(1, 8):
         z_sums(p).start()
-    for p in range(1, 8):
-        z_rows(p).start()
     ring_step(1, 2)
     own[2].wait()
     own[3].wait()

time: 43.5 us -> 43.5 us (level)
  no operation moved by 1% of the time
where the time goes in v5:
time: 43.5 us; the launch traced here: 43.4 us
  Pallas kernels  40.8 us (94%)
  other arithmetic  1.86 us (4%)
  between operations  0.66 us (2%)
    pallas_call x1, Pallas kernels, local(): pl.pallas_call(kernel, out_shape=(block, block, other, other), in_specs=[...  40.8 us
    another operation x1, other arithmetic, local(): jnp.stack([image_emb, text_emb])  1 us

profile of v5, /device:TPU:1, one launch (start us, length us, event | category | flops | bytes accessed | tf_op | source)
XLA Modules:
  0.0 43.4 jit_solution(11861338517207247991)
XLA Ops:
  0.6 0.0 copy-start
  0.6 1.0 %pad_maximum_fusion.both_ref = bf16[2,128,512]{2,1,0:T(8,128)(2,1)S(1)} fusion(bf16[1,128,512]{2,1,0:T(8,128)(2,1)} %bitcast.4, bf16[1,128,512]{2,1,0:T(8,128)(2,1)} %bitcast.5), kind=kLoop, calls=%fused_computation | loop fusion | flops 131072 | bytes 524288 | tf_op jit(solution)/shard_map/stack | solution.py:374
  1.6 0.0 copy-done
  1.7 40.8 %shard_map.50 = (f32[128,512]{1,0:T(8,128)S(1)}, f32[128,512]{1,0:T(8,128)S(1)}, bf16[128,512]{1,0:T(8,128)(2,1)S(1)}, bf16[128,512]{1,0:T(8,128)(2,1)S(1)}) custom-call(bf16[2,128,512]{2,1,0:T(8,128)(2,1)S(1)} %pad_maximum_fusion.both_ref, s32[1,128]{1,0:T(1,128)S(1)} %bitcast.3), custom_call_target="tpu_custom_call" | custom-call | flops 2147483648 | bytes 4194304 | tf_op jit(solution)/shard_map/pallas_call | solution.py:330
  42.5 0.9 %convert_add_fusion = (f32[128,512]{1,0:T(8,128)}, f32[128,512]{1,0:T(8,128)}) fusion(f32[128,512]{1,0:T(8,128)S(1)} %get-tuple-element.8, bf16[128,512]{1,0:T(8,128)(2,1)S(1)} %get-tuple-element.9, f32[128,512]{1,0:T(8,128)S(1)} %get-tuple-element.6, bf16[128,512]{1,0:T(8,128)(2,1)S(1)} %get-tuple-element.7), kind=kLoop, calls=%fused_computation.1 | loop fusion | flops 262144 | bytes 1310720 | tf_op jit(solution)/shard_map/add | solution.py:375
Async XLA Ops:
  0.6 1.0 %copy-start = (s32[128]{0:T(128)S(1)}, s32[128]{0:T(128)}, u32[]{:S(2)}) copy-start(s32[128]{0:T(128)} %param.5) | copy-start | bytes 1540
